TPU v7x, 32 devices: a whole 2x2x4 slice. The times are simulated.
32 devices in a mesh: dp: 8 (over z, y), ctx: 4 (over x, core).
Axes of the slice: x: 2, y: 2, z: 4, core: 2. Of those that a mesh axis runs over, the one named last changes fastest.
Arguments:
- tokens: bfloat16 [12288, 768], P(('dp', 'ctx')), may hold values from -6 to 6
- first_gain: bfloat16 [768], P('dp'), may hold values from 0.25 to 1.75
- first_shift: bfloat16 [768], P('dp'), may hold values from -1.75 to 1.75
- in_weight: bfloat16 [768, 2304], P('dp'), may hold values from -0.21875 to 0.21875
- in_bias: bfloat16 [2, 768], P(None, 'dp'), may hold values from -1.75 to 1.75
- out_weight: bfloat16 [768, 768], P('dp'), may hold values from -2 to 2
- out_bias: bfloat16 [768], P('dp'), may hold values from -1.75 to 1.75
- second_gain: bfloat16 [768], P('dp'), may hold values from 0.25 to 1.75
- second_shift: bfloat16 [768], P('dp'), may hold values from -1.75 to 1.75
- up_weight: bfloat16 [768, 3072], P('dp'), may hold values from -0.21875 to 0.21875
- up_bias: bfloat16 [3072], P('dp'), may hold values from -3 to 3
- down_weight: bfloat16 [3072, 768], P('dp'), may hold values from -0.109375 to 0.109375
- down_bias: bfloat16 [768], P('dp'), may hold values from -1.75 to 1.75
- cotangent: bfloat16 [12288, 768], P(('dp', 'ctx')), may hold values from -6 to 6
Outputs:
- layer_out: bfloat16 [12288, 768], P(('dp', 'ctx'))
- tokens_grad: bfloat16 [12288, 768], P(('dp', 'ctx'))
- first_gain_grad: float32 [768], P('dp')
- first_shift_grad: float32 [768], P('dp')
- in_weight_grad: float32 [768, 2304], P('dp')
- in_bias_grad: float32 [2, 768], P(None, 'dp')
- out_weight_grad: float32 [768, 768], P('dp')
- out_bias_grad: float32 [768], P('dp')
- second_gain_grad: float32 [768], P('dp')
- second_shift_grad: float32 [768], P('dp')
- up_weight_grad: float32 [768, 3072], P('dp')
- up_bias_grad: float32 [3072], P('dp')
- down_weight_grad: float32 [3072, 768], P('dp')
- down_bias_grad: float32 [768], P('dp')
All inputs are finite; a program needn't handle non-finite values.
Results may differ from a plain program's by a relative error of at most 0.018.
Values may be sent and summed in bfloat16 or wider, within the bound.
No kernel may reach another device: no remote copies, remote signals or barrier semaphores. Data moves between devices by JAX's collectives and lax.ppermute only.
A program may use at most 192 MiB of HBM per device.

v0:
```python
import math

import jax
import jax.numpy as jnp
from jax import lax
from jax.sharding import PartitionSpec as P

HEAD_DIM = 64


epsilon = 1e-05
neg_large = -1e30


def layer_norm(values, gain, shift):
    center = values - jnp.mean(values, axis=-1, keepdims=True)
    spread = jnp.mean(center * center, axis=-1, keepdims=True)
    return center * lax.rsqrt(spread + epsilon) * gain + shift


def norm_back(values, gain, shift, upstream):
    result, pullback = jax.vjp(layer_norm, values, gain, shift)
    return pullback(upstream)


def smooth_gate(values):
    return jax.nn.gelu(values, approximate=True)


def forward_block(state, query_heads, query_pos, key_blk, value_blk, key_pos, factor):
    row_max, row_total, accumulated = state
    scores = (
        jnp.einsum("qhd,khd->hqk", query_heads, key_blk, preferred_element_type=jnp.float32)
        * factor
    )
    allowed = (query_pos[:, None] >= key_pos[None, :])[None]
    scores = jnp.where(allowed, scores, neg_large)
    new_max = jnp.maximum(row_max, jnp.max(scores, axis=-1))
    rescale = jnp.exp(row_max - new_max)
    weights = jnp.where(allowed, jnp.exp(scores - new_max[:, :, None]), 0.0)
    row_total = row_total * rescale + jnp.sum(weights, axis=-1)
    update = jnp.einsum(
        "hqk,khd->qhd", weights.astype(jnp.bfloat16), value_blk, preferred_element_type=jnp.float32
    )
    accumulated = accumulated * rescale.T[:, :, None] + update
    return (new_max, row_total, accumulated)


def pair_grads(
    query_heads, grad_heads, stats, deltas, query_pos, key_blk, value_blk, key_pos, factor
):
    scores = (
        jnp.einsum("qhd,khd->hqk", query_heads, key_blk, preferred_element_type=jnp.float32)
        * factor
    )
    allowed = (query_pos[:, None] >= key_pos[None, :])[None]
    probs = jnp.where(allowed, jnp.exp(scores - stats[:, :, None]), 0.0)
    grad_probs = jnp.einsum(
        "qhd,khd->hqk", grad_heads, value_blk, preferred_element_type=jnp.float32
    )
    grad_scores = (probs * (grad_probs - deltas[:, :, None])).astype(jnp.bfloat16)
    grad_query = (
        jnp.einsum("hqk,khd->qhd", grad_scores, key_blk, preferred_element_type=jnp.float32)
        * factor
    )
    grad_key = (
        jnp.einsum("hqk,qhd->khd", grad_scores, query_heads, preferred_element_type=jnp.float32)
        * factor
    )
    grad_value = jnp.einsum(
        "hqk,qhd->khd", probs.astype(jnp.bfloat16), grad_heads, preferred_element_type=jnp.float32
    )
    return (grad_query, grad_key, grad_value)


def over_keys(state, key_part, value_part, begin_row, top_query, place, block_fn):
    amount, head_count, head_dim = key_part.shape
    stride = math.gcd(amount, 512)
    key_blocks = key_part.reshape(amount // stride, stride, head_count, head_dim)
    value_blocks = value_part.reshape(amount // stride, stride, head_count, head_dim)
    offsets = begin_row + jnp.arange(amount // stride, dtype=jnp.int32) * stride

    def over_step_fn(inner, operands):
        key_blk, value_blk, offset = operands
        key_pos = place(offset + jnp.arange(stride, dtype=jnp.int32))

        def over_compute(current):
            return block_fn(current, key_blk, value_blk, key_pos)

        def keep(current):
            return current

        return (lax.cond(jnp.min(key_pos) <= top_query, over_compute, keep, inner), None)

    state, unused = lax.scan(over_step_fn, state, (key_blocks, value_blocks, offsets))
    return state


def body(
    tokens,
    first_gain,
    first_shift,
    in_weight,
    in_bias,
    out_weight,
    out_bias,
    second_gain,
    second_shift,
    up_weight,
    up_bias,
    down_weight,
    down_bias,
    cotangent,
):
    (
        first_gain,
        first_shift,
        in_weight,
        in_bias,
        out_weight,
        out_bias,
        second_gain,
        second_shift,
        up_weight,
        up_bias,
        down_weight,
        down_bias,
    ) = (
        lax.all_gather(first_gain, "dp", axis=0, tiled=True),
        lax.all_gather(first_shift, "dp", axis=0, tiled=True),
        lax.all_gather(in_weight, "dp", axis=0, tiled=True),
        lax.all_gather(in_bias, "dp", axis=1, tiled=True),
        lax.all_gather(out_weight, "dp", axis=0, tiled=True),
        lax.all_gather(out_bias, "dp", axis=0, tiled=True),
        lax.all_gather(second_gain, "dp", axis=0, tiled=True),
        lax.all_gather(second_shift, "dp", axis=0, tiled=True),
        lax.all_gather(up_weight, "dp", axis=0, tiled=True),
        lax.all_gather(up_bias, "dp", axis=0, tiled=True),
        lax.all_gather(down_weight, "dp", axis=0, tiled=True),
        lax.all_gather(down_bias, "dp", axis=0, tiled=True),
    )
    rows_dev = tokens.shape[0]
    width = tokens.shape[1]
    head_dim = HEAD_DIM
    head_count = width // head_dim
    factor = 1.0 / math.sqrt(head_dim)
    my_index = lax.axis_index("ctx")

    def place(rows):
        return rows

    query_pos = place(my_index * rows_dev + jnp.arange(rows_dev, dtype=jnp.int32))
    top_query = jnp.max(query_pos)
    inputs = tokens.astype(jnp.float32)
    gain_one = first_gain.astype(jnp.float32)
    shift_one = first_shift.astype(jnp.float32)
    first_low = layer_norm(inputs, gain_one, shift_one).astype(jnp.bfloat16)
    bias_full = jnp.concatenate([in_bias[0], jnp.zeros((width,), jnp.bfloat16), in_bias[1]]).astype(
        jnp.float32
    )
    mixture = (
        jnp.dot(first_low, in_weight, preferred_element_type=jnp.float32) + bias_full
    ).astype(jnp.bfloat16)
    query_rows = mixture[:, :width]
    key_rows = mixture[:, width : 2 * width]
    value_rows = mixture[:, 2 * width :]
    query_heads = query_rows.reshape(rows_dev, head_count, head_dim)

    def forward_fold(state, portion, begin_row):
        key_part, value_part = portion
        amount = key_part.shape[0]

        def block_fn(inner, key_blk, value_blk, key_pos):
            return forward_block(inner, query_heads, query_pos, key_blk, value_blk, key_pos, factor)

        return over_keys(
            state,
            key_part.reshape(amount, head_count, head_dim),
            value_part.reshape(amount, head_count, head_dim),
            begin_row,
            top_query,
            place,
            block_fn,
        )

    start_state = (
        jnp.full((head_count, rows_dev), neg_large, jnp.float32),
        jnp.zeros((head_count, rows_dev), jnp.float32),
        jnp.zeros((rows_dev, head_count, head_dim), jnp.float32),
    )
    row_max, row_total, accumulated = forward_fold(
        start_state,
        (
            lax.all_gather(key_rows, "ctx", axis=0, tiled=True),
            lax.all_gather(value_rows, "ctx", axis=0, tiled=True),
        ),
        jnp.int32(0),
    )
    stats = row_max + jnp.log(row_total)
    context_heads = accumulated / row_total.T[:, :, None]
    context_low = context_heads.reshape(rows_dev, width).astype(jnp.bfloat16)
    residual = (
        inputs
        + jnp.dot(context_low, out_weight, preferred_element_type=jnp.float32)
        + out_bias.astype(jnp.float32)
    )
    gain_two = second_gain.astype(jnp.float32)
    shift_two = second_shift.astype(jnp.float32)
    second_low = layer_norm(residual, gain_two, shift_two).astype(jnp.bfloat16)
    hidden = jnp.dot(second_low, up_weight, preferred_element_type=jnp.float32) + up_bias.astype(
        jnp.float32
    )
    activated, gate_back = jax.vjp(smooth_gate, hidden)
    active_low = activated.astype(jnp.bfloat16)
    layer_out = (
        residual
        + jnp.dot(active_low, down_weight, preferred_element_type=jnp.float32)
        + down_bias.astype(jnp.float32)
    ).astype(jnp.bfloat16)
    upstream = cotangent.astype(jnp.float32)
    down_bias_grad = jnp.sum(upstream, axis=0)
    down_weight_grad = jnp.einsum(
        "tf,td->fd", active_low, cotangent, preferred_element_type=jnp.float32
    )
    (grad_hidden,) = gate_back(
        jnp.einsum("td,fd->tf", cotangent, down_weight, preferred_element_type=jnp.float32)
    )
    grad_hidden = grad_hidden.astype(jnp.bfloat16)
    up_weight_grad = jnp.einsum(
        "td,tf->df", second_low, grad_hidden, preferred_element_type=jnp.float32
    )
    up_bias_grad = jnp.sum(grad_hidden.astype(jnp.float32), axis=0)
    grad_second = jnp.einsum(
        "tf,df->td", grad_hidden, up_weight, preferred_element_type=jnp.float32
    )
    grad_residual, second_gain_grad, second_shift_grad = norm_back(
        residual, gain_two, shift_two, grad_second
    )
    grad_residual = grad_residual + upstream
    grad_attn = grad_residual.astype(jnp.bfloat16)
    out_bias_grad = jnp.sum(grad_attn.astype(jnp.float32), axis=0)
    out_weight_grad = jnp.einsum(
        "td,te->de", context_low, grad_attn, preferred_element_type=jnp.float32
    )
    grad_context = jnp.einsum(
        "te,de->td", grad_attn, out_weight, preferred_element_type=jnp.float32
    ).astype(jnp.bfloat16)
    grad_heads = grad_context.reshape(rows_dev, head_count, head_dim)
    deltas = jnp.sum(grad_heads.astype(jnp.float32) * context_heads, axis=-1).T

    def query_fold(state, portion, begin_row):
        key_part, value_part = portion
        amount = key_part.shape[0]

        def block_fn(inner, key_blk, value_blk, key_pos):
            grad_query, grad_key, grad_value = pair_grads(
                query_heads,
                grad_heads,
                stats,
                deltas,
                query_pos,
                key_blk,
                value_blk,
                key_pos,
                factor,
            )
            return inner + grad_query

        return over_keys(
            state,
            key_part.reshape(amount, head_count, head_dim),
            value_part.reshape(amount, head_count, head_dim),
            begin_row,
            top_query,
            place,
            block_fn,
        )

    zero_heads = jnp.zeros((rows_dev, head_count, head_dim), jnp.float32)
    key_all, value_all = (
        lax.all_gather(key_rows, "ctx", axis=0, tiled=True),
        lax.all_gather(value_rows, "ctx", axis=0, tiled=True),
    )
    grad_query = query_fold(zero_heads, (key_all, value_all), 0)
    amount = lax.axis_size("ctx") * rows_dev
    stride = math.gcd(amount, 512)
    key_part = key_all.reshape(amount // stride, stride, head_count, head_dim)
    value_part = value_all.reshape(amount // stride, stride, head_count, head_dim)
    offsets = jnp.arange(amount // stride, dtype=jnp.int32) * stride

    def key_step_fn(unused, operands):
        key_blk, value_blk, offset = operands
        key_pos = place(offset + jnp.arange(stride, dtype=jnp.int32))

        def key_compute(blocks_in):
            grad_query_part, grad_key, grad_value = pair_grads(
                query_heads,
                grad_heads,
                stats,
                deltas,
                query_pos,
                blocks_in[0],
                blocks_in[1],
                key_pos,
                factor,
            )
            return jnp.concatenate(
                [grad_key.reshape(stride, width), grad_value.reshape(stride, width)], axis=1
            )

        def nothing(blocks_in):
            return jnp.zeros((stride, 2 * width), jnp.float32)

        return (
            unused,
            lax.cond(jnp.min(key_pos) <= top_query, key_compute, nothing, (key_blk, value_blk)),
        )

    unused, stacked = lax.scan(key_step_fn, 0, (key_part, value_part, offsets))
    grad_pairs = lax.psum_scatter(
        stacked.reshape(amount, 2 * width).astype(jnp.bfloat16),
        "ctx",
        scatter_dimension=0,
        tiled=True,
    ).astype(jnp.float32)
    grad_key = grad_pairs[:, :width]
    grad_value = grad_pairs[:, width:]
    grad_mixture = jnp.concatenate(
        [grad_query.reshape(rows_dev, width), grad_key, grad_value], axis=1
    ).astype(jnp.bfloat16)
    in_weight_grad = jnp.einsum(
        "td,te->de", first_low, grad_mixture, preferred_element_type=jnp.float32
    )
    in_bias_grad = jnp.stack(
        [
            jnp.sum(grad_mixture[:, :width].astype(jnp.float32), axis=0),
            jnp.sum(grad_mixture[:, 2 * width :].astype(jnp.float32), axis=0),
        ]
    )
    grad_first = jnp.einsum(
        "te,de->td", grad_mixture, in_weight, preferred_element_type=jnp.float32
    )
    grad_inputs, first_gain_grad, first_shift_grad = norm_back(
        inputs, gain_one, shift_one, grad_first
    )
    tokens_grad = (grad_inputs + grad_residual).astype(jnp.bfloat16)
    (
        first_gain_grad,
        first_shift_grad,
        in_weight_grad,
        in_bias_grad,
        out_weight_grad,
        out_bias_grad,
        second_gain_grad,
        second_shift_grad,
        up_weight_grad,
        up_bias_grad,
        down_weight_grad,
        down_bias_grad,
    ) = (
        lax.psum_scatter(
            first_gain_grad.astype(jnp.bfloat16), "dp", scatter_dimension=0, tiled=True
        ).astype(jnp.float32),
        lax.psum_scatter(
            first_shift_grad.astype(jnp.bfloat16), "dp", scatter_dimension=0, tiled=True
        ).astype(jnp.float32),
        lax.psum_scatter(
            in_weight_grad.astype(jnp.bfloat16), "dp", scatter_dimension=0, tiled=True
        ).astype(jnp.float32),
        lax.psum_scatter(
            in_bias_grad.astype(jnp.bfloat16), "dp", scatter_dimension=1, tiled=True
        ).astype(jnp.float32),
        lax.psum_scatter(
            out_weight_grad.astype(jnp.bfloat16), "dp", scatter_dimension=0, tiled=True
        ).astype(jnp.float32),
        lax.psum_scatter(
            out_bias_grad.astype(jnp.bfloat16), "dp", scatter_dimension=0, tiled=True
        ).astype(jnp.float32),
        lax.psum_scatter(
            second_gain_grad.astype(jnp.bfloat16), "dp", scatter_dimension=0, tiled=True
        ).astype(jnp.float32),
        lax.psum_scatter(
            second_shift_grad.astype(jnp.bfloat16), "dp", scatter_dimension=0, tiled=True
        ).astype(jnp.float32),
        lax.psum_scatter(
            up_weight_grad.astype(jnp.bfloat16), "dp", scatter_dimension=0, tiled=True
        ).astype(jnp.float32),
        lax.psum_scatter(
            up_bias_grad.astype(jnp.bfloat16), "dp", scatter_dimension=0, tiled=True
        ).astype(jnp.float32),
        lax.psum_scatter(
            down_weight_grad.astype(jnp.bfloat16), "dp", scatter_dimension=0, tiled=True
        ).astype(jnp.float32),
        lax.psum_scatter(
            down_bias_grad.astype(jnp.bfloat16), "dp", scatter_dimension=0, tiled=True
        ).astype(jnp.float32),
    )
    (
        first_gain_grad,
        first_shift_grad,
        in_weight_grad,
        in_bias_grad,
        out_weight_grad,
        out_bias_grad,
        second_gain_grad,
        second_shift_grad,
        up_weight_grad,
        up_bias_grad,
        down_weight_grad,
        down_bias_grad,
    ) = (
        lax.psum(first_gain_grad.astype(jnp.bfloat16), "ctx").astype(jnp.float32),
        lax.psum(first_shift_grad.astype(jnp.bfloat16), "ctx").astype(jnp.float32),
        lax.psum(in_weight_grad.astype(jnp.bfloat16), "ctx").astype(jnp.float32),
        lax.psum(in_bias_grad.astype(jnp.bfloat16), "ctx").astype(jnp.float32),
        lax.psum(out_weight_grad.astype(jnp.bfloat16), "ctx").astype(jnp.float32),
        lax.psum(out_bias_grad.astype(jnp.bfloat16), "ctx").astype(jnp.float32),
        lax.psum(second_gain_grad.astype(jnp.bfloat16), "ctx").astype(jnp.float32),
        lax.psum(second_shift_grad.astype(jnp.bfloat16), "ctx").astype(jnp.float32),
        lax.psum(up_weight_grad.astype(jnp.bfloat16), "ctx").astype(jnp.float32),
        lax.psum(up_bias_grad.astype(jnp.bfloat16), "ctx").astype(jnp.float32),
        lax.psum(down_weight_grad.astype(jnp.bfloat16), "ctx").astype(jnp.float32),
        lax.psum(down_bias_grad.astype(jnp.bfloat16), "ctx").astype(jnp.float32),
    )
    return (
        layer_out,
        tokens_grad,
        first_gain_grad,
        first_shift_grad,
        in_weight_grad,
        in_bias_grad,
        out_weight_grad,
        out_bias_grad,
        second_gain_grad,
        second_shift_grad,
        up_weight_grad,
        up_bias_grad,
        down_weight_grad,
        down_bias_grad,
    )


def solution(mesh):
    in_specs = (
        P(("dp", "ctx"), None),
        P("dp"),
        P("dp"),
        P("dp", None),
        P(None, "dp"),
        P("dp", None),
        P("dp"),
        P("dp"),
        P("dp"),
        P("dp", None),
        P("dp"),
        P("dp", None),
        P("dp"),
        P(("dp", "ctx"), None),
    )
    out_specs = (
        P(("dp", "ctx"), None),
        P(("dp", "ctx"), None),
        P("dp"),
        P("dp"),
        P("dp", None),
        P(None, "dp"),
        P("dp", None),
        P("dp"),
        P("dp"),
        P("dp"),
        P("dp", None),
        P("dp"),
        P("dp", None),
        P("dp"),
    )
    return jax.shard_map(body, mesh=mesh, in_specs=in_specs, out_specs=out_specs, check_vma=False)
```

profile of v0, /device:TPU:0, one launch (start us, length us, event | category | flops | bytes accessed | tf_op | source)
XLA Modules:
  0.0 950.9 jit_solution(6833802407159775218)
XLA Ops:
  14.9 39.6 %all-reduce.14 = (bf16[768]{0:T(1024)(128)(2,1)S(1)}, bf16[768]{0:T(1024)(128)(2,1)S(1)}, bf16[768]{0:T(1024)(128)(2,1)S(1)}, bf16[768]{0:T(1024)(128)(2,1)S(1)}, bf16[768]{0:T(1024)(128)(2,1)S(1)}) all-reduce(bf16[768]{0:T(1024)(128)(2,1)S(1)} %dynamic-update-slice.1, ...), channel_id=1, replica_groups=mesh['dp'=8,'ctx'=4] {'dp'}, use_global_device_ids=true, to_apply=%add.1 | all-reduce | flops 3840 | bytes 15360
  54.5 16.6 %all-gather = bf16[8,96,2]{1,2,0:T(2,128)(2,1)S(1)} all-gather(bf16[1,96,2]{1,2,0:T(2,128)(2,1)} %bitcast.159), channel_id=1, replica_groups=mesh['dp'=8,'ctx'=4] {'dp'}, dimensions={0}, use_global_device_ids=true | all-gather | bytes 3456 | tf_op jit(solution)/shard_map/all_gather | solution.py:132
  86.0 26.5 %all-gather.1 = bf16[8,1,384]{2,1,0:T(2,128)(2,1)S(1)} all-gather(bf16[1,1,384]{2,1,0:T(2,128)(2,1)S(1)} %reshape.253), channel_id=1, replica_groups=mesh['dp'=8,'ctx'=4] {'dp'}, dimensions={0}, use_global_device_ids=true | all-gather | bytes 6912 | tf_op jit(solution)/shard_map/all_gather | solution.py:138
  113.6 45.9 %all-gather.19.cloned.1.call-done = bf16[3072,768]{1,0:T(8,128)(2,1)} async-done(((bf16[384,768]{1,0:T(8,128)(2,1)}), bf16[3072,768]{1,0:T(8,128)(2,1)}) %all-gather.19.cloned.1.call-update) | async-done | bytes 4718608 | tf_op jit(solution)/shard_map/all_gather | solution.py:139
  159.5 6.5 fusion.130
  166.1 17.9 %all-gather.11.cloned.1.call-done = bf16[1536,768]{1,0:T(8,128)(2,1)} async-done(((bf16[384,768]{1,0:T(8,128)(2,1)}), bf16[1536,768]{1,0:T(8,128)(2,1)}) %all-gather.11.cloned.1.call-update) | async-done | bytes 2359312 | tf_op jit(solution)/shard_map/all_gather | solution.py:194
  183.9 8.4 reshape.277
  192.3 7.5 copy.84
  199.7 10.3 %all-gather.13.cloned.1.call-done = bf16[1536,768]{1,0:T(8,128)(2,1)} async-done(((bf16[384,768]{1,0:T(8,128)(2,1)}), bf16[1536,768]{1,0:T(8,128)(2,1)}) %all-gather.13.cloned.1.call-update) | async-done | bytes 2359312 | tf_op jit(solution)/shard_map/all_gather | solution.py:195
  210.0 8.2 reshape.278
  218.2 7.4 copy.85
  225.7 18.8 %while.40 = (s32[]{:T(128)}, f32[12,384]{1,0:T(8,128)S(1)}, f32[12,384]{1,0:T(8,128)S(1)}, f32[384,12,64]{0,2,1:T(8,128)S(1)}, s32[3]{0:T(128)S(1)}, /*index=5*/...) while((s32[]{:T(128)}, f32[12,384]{1,0:T(8,128)S(1)}, ...), condition=%wide.region_9.10_spmd.clone, body=%wide.region_3.9_spmd.clone.sunk | while | flops 635452288 | bytes 33926424 | solution.py:95
  228.9 9.2 conditional.9
  245.5 7.7 all-gather.15.cloned.1.call-done
  255.6 78.2 %all-gather.17.cloned.1.call-done = bf16[768,3072]{1,0:T(8,128)(2,1)} async-done(((bf16[96,3072]{1,0:T(8,128)(2,1)}), bf16[768,3072]{1,0:T(8,128)(2,1)}) %all-gather.17.cloned.1.call-update) | async-done | bytes 4718608 | tf_op jit(solution)/shard_map/all_gather | solution.py:137
  333.9 11.1 %fusion.122 = (bf16[3072]{0:T(1024)(128)(2,1)}, bf16[384,3072]{1,0:T(8,128)(2,1)S(1)}, f32[384,3072]{1,0:T(8,128)}) fusion(f32[384,3072]{1,0:T(8,128)} %fusion.130, f32[3072]{0:T(1024)S(1)} %bitcast.158, bf16[768,3072]{1,0:T(8,128)(2,1)} %all-gather.17.cloned.1.call-done, f32[384,768]{1,0:T(8,128)S(1)} %get-tuple-element.769, ...), kind=kOutput, calls=%fused_computation.153 | convolution fusion | flops 1839363072 | bytes 17722368 | tf_op jit(solution)/shard_map/dot_general | solution.py:210
  353.4 36.2 %while.42 = (s32[]{:T(128)}, bf16[3,512,1536]{2,1,0:T(8,128)(2,1)}, s32[3]{0:T(128)S(1)}, s32[]{:T(128)}, bf16[3,512,12,64]{1,3,2,0:T(8,128)(2,1)}, /*index=5*/b...) while((s32[]{:T(128)}, bf16[3,512,1536]{2,1,0:T(8,128)(2,1)}, ...), condition=%wide.region_24.25_spmd.clone, body=%wide.region_20.0_spmd.clone.sunk | while | flops 1235682688 | bytes 43910896 | solution.py:319
  356.5 20.5 %conditional.11 = (bf16[1,512,1536]{1,2,0:T(8,128)(2,1)S(1)}) conditional(s32[]{:T(128)} %convert_element_type.345, () %tuple.143, (s32[]{:T(128)}, s32[512]{0:T(512)S(1)}, bf16[3,512,12,64]{1,3,2,0:T(8,128)(2,1)}, s32[]{:T(128)}, bf16[384,12,64]{0,2,1:T(8,128)(2,1)}, /*index=5*/f32[12,384]{1,0:T(8,128)S(1)}, bf16[3,512,12,64]{1,3,2,0:T(8,128)(2,1)}, ...), branch_computations={%region_22.22_spmd, %region_23.23_spmd} | conditional | flops 1235681664 | bytes 37615116 | solution.py:316
  363.1 8.0 fusion.68
  400.3 7.5 convolution_convert_fusion
  408.5 24.2 %while.41 = (s32[]{:T(128)}, f32[384,12,64]{0,2,1:T(8,128)S(1)}, s32[3]{0:T(128)S(1)}, s32[]{:T(128)}, bf16[3,512,12,64]{1,3,2,0:T(8,128)(2,1)}, /*index=5*/bf16...) while((s32[]{:T(128)}, f32[384,12,64]{0,2,1:T(8,128)S(1)}, ...), condition=%wide.region_19.20_spmd.clone, body=%wide.region_15.0_spmd.clone.sunk | while | flops 920913280 | bytes 25214716 | solution.py:95
  411.6 14.7 %conditional.10 = (f32[384,12,64]{0,2,1:T(8,128)S(1)}) conditional(s32[]{:T(128)} %convert_element_type.344, f32[384,12,64]{0,2,1:T(8,128)S(1)} %get-tuple-element.1074, (s32[]{:T(128)}, s32[512]{0:T(512)S(1)}, bf16[3,512,12,64]{1,3,2,0:T(8,128)(2,1)}, s32[]{:T(128)}, bf16[384,12,64]{0,2,1:T(8,128)(2,1)}, /*index=5*/f32[12,384]{1,0:T(8,128)S(1)}, ...), branch_computations={%region_17.17_spmd, %region_18.18_spmd} | conditional | flops 920912256 | bytes 25210892 | solution.py:93
  418.2 8.1 fusion.41
  433.2 43.2 %reduce-scatter.9.cloned.1.call-done = bf16[384,1536]{1,0:T(8,128)(2,1)} async-done(((bf16[1536,1536]{1,0:T(8,128)(2,1)}), bf16[384,1536]{1,0:T(8,128)(2,1)}) %reduce-scatter.9.cloned.1.call-update) | async-done | bytes 1179664 | tf_op jit(solution)/shard_map/reduce_scatter | solution.py:320
  494.9 38.1 %all-reduce.13 = (bf16[768]{0:T(1024)(128)(2,1)S(1)}, bf16[768]{0:T(1024)(128)(2,1)S(1)}, bf16[768]{0:T(1024)(128)(2,1)S(1)}, bf16[768]{0:T(1024)(128)(2,1)S(1)}...) all-reduce(bf16[768]{0:T(1024)(128)(2,1)} %copy-done.30, ...), channel_id=1, replica_groups=mesh['dp'=8,'ctx'=4] {'dp'}, use_global_device_ids=true, to_apply=%add.5 | all-reduce | flops 8448 | bytes 33792
  533.5 10.8 %reduce-scatter.13.cloned.1.call-done = bf16[96,768]{1,0:T(8,128)(2,1)} async-done(((bf16[768,768]{1,0:T(8,128)(2,1)}), bf16[96,768]{1,0:T(8,128)(2,1)}) %reduce-scatter.13.cloned.1.call-update) | async-done | bytes 147472 | tf_op jit(solution)/shard_map/reduce_scatter | solution.py:373
  544.3 98.5 %reduce-scatter.15.cloned.1.call-done = bf16[96,3072]{1,0:T(8,128)(2,1)} async-done(((bf16[768,3072]{1,0:T(8,128)(2,1)}), bf16[96,3072]{1,0:T(8,128)(2,1)}) %reduce-scatter.15.cloned.1.call-update) | async-done | bytes 589840 | tf_op jit(solution)/shard_map/reduce_scatter | solution.py:385
  642.9 99.1 %reduce-scatter.17.cloned.1.call-done = bf16[384,768]{1,0:T(8,128)(2,1)} async-done(((bf16[3072,768]{1,0:T(8,128)(2,1)}), bf16[384,768]{1,0:T(8,128)(2,1)}) %reduce-scatter.17.cloned.1.call-update) | async-done | bytes 589840 | tf_op jit(solution)/shard_map/reduce_scatter | solution.py:391
  742.0 82.8 %reduce-scatter.11.cloned.1.call-done = bf16[96,2304]{1,0:T(8,128)(2,1)} async-done(((bf16[768,2304]{1,0:T(8,128)(2,1)}), bf16[96,2304]{1,0:T(8,128)(2,1)}) %reduce-scatter.11.cloned.1.call-update) | async-done | bytes 442384 | tf_op jit(solution)/shard_map/reduce_scatter | solution.py:367
  824.9 7.4 fusion.104
  832.3 57.3 %reduce-scatter.19.cloned.1.call-done = bf16[96,2]{1,0:T(8,128)(2,1)} async-done(((bf16[768,2]{1,0:T(8,128)(2,1)}), bf16[96,2]{1,0:T(8,128)(2,1)}) %reduce-scatter.19.cloned.1.call-update) | async-done | bytes 400
  900.4 37.7 %all-reduce.19.cloned.1.call-done = (bf16[96,2304]{1,0:T(8,128)(2,1)}, bf16[96,768]{1,0:T(8,128)(2,1)}, bf16[96,3072]{1,0:T(8,128)(2,1)}, bf16[384,768]{1,0:T(8,128)(2,1)}) async-done(((bf16[96,2304]{1,0:T(8,128)(2,1)}, bf16[96,768]{1,0:T(8,128)(2,1)}, bf16[96,3072]{1,0:T(8,128)(2,1)}, bf16[384,768]{1,0:T(8,128)(2,1)}), (bf16[96,2304]{1,0:T(8,128)(2,1)}, bf16[96,768]{1,0:T(8,128)(2,1)}, ...) | async-done | bytes 1769488 | tf_op jit(solution)/shard_map/psum | solution.py:414
  (248 shorter events, 132.2 us)
Async XLA Ops:
  7.2 71.5 %copy-start.2 = (bf16[384,768]{1,0:T(8,128)(2,1)S(1)}, bf16[384,768]{1,0:T(8,128)(2,1)}, u32[]{:S(2)}) copy-start(bf16[384,768]{1,0:T(8,128)(2,1)} %param.26) | copy-start | bytes 1769476
  7.2 71.5 %all-gather.9.cloned.1.call-start = ((), (), s32[]{:S(2)}) async-start(), calls=%async_computation.6 | async-start | bytes 3981312 | tf_op jit(solution)/shard_map/all_gather | solution.py:131
  7.9 151.6 %all-gather.19.cloned.1.call-start = ((), (), s32[]{:S(2)}) async-start(), calls=%async_computation.11 | async-start | bytes 5308416 | tf_op jit(solution)/shard_map/all_gather | solution.py:139
  8.7 175.2 %all-gather.11.cloned.1.call-start = ((), (), s32[]{:S(2)}) async-start(), calls=%async_computation.7 | async-start | bytes 2949120 | tf_op jit(solution)/shard_map/all_gather | solution.py:194
  54.5 27.8 %copy-start.17 = (f32[768]{0:T(1024)}, f32[768]{0:T(1024)S(1)}, u32[]{:S(2)}) copy-start(f32[768]{0:T(1024)S(1)} %convert_element_type.204) | copy-start | bytes 9220
  54.5 27.8 %copy-start.31 = (f32[768]{0:T(1024)}, f32[768]{0:T(1024)S(1)}, u32[]{:S(2)}) copy-start(f32[768]{0:T(1024)S(1)} %convert_element_type.205) | copy-start | bytes 9220
  72.5 9.9 %copy-start.19 = (f32[384]{0:T(512)}, f32[384]{0:T(512)S(1)}, u32[]{:S(2)}) copy-start(f32[384]{0:T(512)S(1)} %broadcast_multiply_fusion.1) | copy-start | bytes 4612
  73.8 8.5 copy-start.25
  73.9 8.5 copy-start.27
  82.4 3.6 copy-start.32
  83.5 76.0 %copy-start.8 = (bf16[384,768]{1,0:T(8,128)(2,1)S(1)}, bf16[384,768]{1,0:T(8,128)(2,1)}, u32[]{:S(2)}) copy-start(bf16[384,768]{1,0:T(8,128)(2,1)} %param.39) | copy-start | bytes 1769476
  83.5 126.5 %all-gather.13.cloned.1.call-start = ((), (), s32[]{:S(2)}) async-start(), calls=%async_computation.8 | async-start | bytes 2949120 | tf_op jit(solution)/shard_map/all_gather | solution.py:195
  84.1 169.0 %all-gather.15.cloned.1.call-start = ((), (), s32[]{:S(2)}) async-start(), calls=%async_computation.9 | async-start | bytes 1327104 | tf_op jit(solution)/shard_map/all_gather | solution.py:133
  84.7 249.1 %all-gather.17.cloned.1.call-start = ((), (), s32[]{:S(2)}) async-start(), calls=%async_computation.10 | async-start | bytes 5308416 | tf_op jit(solution)/shard_map/all_gather | solution.py:137
  85.3 391.2 %reduce-scatter.9.cloned.1.call-start = ((), (), s32[]{:S(2)}) async-start(), calls=%async_computation.12 | async-start | bytes 5898240 | tf_op jit(solution)/shard_map/reduce_scatter | solution.py:320
  255.4 92.5 %copy-start.4 = (f32[384,768]{1,0:T(8,128)}, f32[384,768]{1,0:T(8,128)S(1)}, u32[]{:S(2)}) copy-start(f32[384,768]{1,0:T(8,128)S(1)} %get-tuple-element.769) | copy-start | bytes 3538948
  333.9 11.1 %copy-start.33 = (bf16[768,3072]{1,0:T(8,128)(2,1)S(1)}, bf16[768,3072]{1,0:T(8,128)(2,1)}, u32[]{:S(2)}) copy-start(bf16[768,3072]{1,0:T(8,128)(2,1)} %all-gather.17.cloned.1.call-done) | copy-start | bytes 14155780
  350.3 3.0 copy-start.12
  390.2 154.1 %reduce-scatter.13.cloned.1.call-start = ((), (), s32[]{:S(2)}) async-start(), calls=%async_computation.14 | async-start | bytes 1327104 | tf_op jit(solution)/shard_map/reduce_scatter | solution.py:373
  392.7 250.1 %reduce-scatter.15.cloned.1.call-start = ((), (), s32[]{:S(2)}) async-start(), calls=%async_computation.15 | async-start | bytes 5308416 | tf_op jit(solution)/shard_map/reduce_scatter | solution.py:385
  399.2 342.8 %reduce-scatter.17.cloned.1.call-start = ((), (), s32[]{:S(2)}) async-start(), calls=%async_computation.16 | async-start | bytes 5308416 | tf_op jit(solution)/shard_map/reduce_scatter | solution.py:391
  407.8 417.1 %reduce-scatter.11.cloned.1.call-start = ((), (), s32[]{:S(2)}) async-start(), calls=%async_computation.13 | async-start | bytes 3981312 | tf_op jit(solution)/shard_map/reduce_scatter | solution.py:367
  432.7 43.7 %copy-start.3 = (bf16[384,768]{1,0:T(8,128)(2,1)S(1)}, bf16[384,768]{1,0:T(8,128)(2,1)}, u32[]{:S(2)}) copy-start(bf16[384,768]{1,0:T(8,128)(2,1)} %param.26) | copy-start | bytes 1769476
  432.7 43.7 %copy-start.18 = (f32[768]{0:T(1024)S(1)}, f32[768]{0:T(1024)}, u32[]{:S(2)}) copy-start(f32[768]{0:T(1024)} %copy-done.17) | copy-start | bytes 9220
  432.7 43.7 %copy-start.20 = (f32[384]{0:T(512)S(1)}, f32[384]{0:T(512)}, u32[]{:S(2)}) copy-start(f32[384]{0:T(512)} %copy-done.19) | copy-start | bytes 4612
  432.8 43.7 %copy-start.28 = (f32[384]{0:T(512)S(1)}, f32[384]{0:T(512)}, u32[]{:S(2)}) copy-start(f32[384]{0:T(512)} %copy-done.27) | copy-start | bytes 4612
  481.8 407.8 %reduce-scatter.19.cloned.1.call-start = ((), (), s32[]{:S(2)}) async-start(), calls=%async_computation.17 | async-start | bytes 221184
  485.1 4.3 copy-start.26
  492.1 332.8 %copy-start.6 = (f32[384,768]{1,0:T(8,128)S(1)}, f32[384,768]{1,0:T(8,128)}, u32[]{:S(2)}) copy-start(f32[384,768]{1,0:T(8,128)} %copy-done.4) | copy-start | bytes 3538948
  492.1 445.9 %all-reduce.19.cloned.1.call-start = ((), (), s32[]{:S(2)}) async-start(), calls=%async_computation.18 | async-start | bytes 3538944 | tf_op jit(solution)/shard_map/psum | solution.py:414
  938.0 4.4 copy-start.14
  938.0 5.4 copy-start.16
  (18 other events, 27.4 us)
Sparse Core Ops, SparseCore 0:
  10.2 68.3 all-gather.8
  80.8 78.6 all-gather.18
  161.7 22.1 all-gather.10
  185.9 24.0 all-gather.12
  212.0 41.0 all-gather.14
  255.2 78.6 all-gather.16
  389.8 86.6 reduce-scatter.8
  480.2 64.0 reduce-scatter.12
  548.4 94.4 reduce-scatter.14
  646.8 95.1 reduce-scatter.16
  746.1 78.7 reduce-scatter.10
  828.9 60.6 reduce-scatter.18
  892.4 45.6 all-reduce.18
where the time goes:
time: 958 us; the launch traced here: 951 us
  waiting for transfers between devices  597 us (62%)
  blocking collectives  127 us (13%)
  matrix products  101 us (11%)
  local copies, waits for them, and re-layouts  60.2 us (6%)
  other arithmetic  36.6 us (4%)
  between operations  16.6 us (2%)
  loops' own time  12.1 us (1%)
    reduce_scatter x1, waiting for transfers between devices, body(): lax.psum_scatter(down_weight_grad.astype(jnp.bfloat16), 'dp', scatter_dim...  99.1 us
    reduce_scatter x1, waiting for transfers between devices, body(): lax.psum_scatter(up_weight_grad.astype(jnp.bfloat16), 'dp', scatter_dimen...  98.5 us
    reduce_scatter x1, waiting for transfers between devices, body(): lax.psum_scatter(in_weight_grad.astype(jnp.bfloat16), 'dp', scatter_dimen...  82.8 us
    all_gather x1, waiting for transfers between devices, body(): lax.all_gather(up_weight, 'dp', axis=0, tiled=True)  78.2 us
    unnamed x2, blocking collectives  77.7 us
    unnamed x14, waiting for transfers between devices  60.4 us
    all_gather x1, waiting for transfers between devices, body(): lax.all_gather(down_weight, 'dp', axis=0, tiled=True)  45.9 us
    reduce_scatter x1, waiting for transfers between devices, body(): lax.psum_scatter(stacked.reshape(amount, 2 * width).astype(jnp.bfloat16),...  43.2 us
  transfers between devices with their start and end apart: 13, of which 13 were waited for; matrix products, arithmetic and copies ran while one was open for 14% of the time, Pallas kernels for 0%

commit v1 on v0

--- a/solution.py
+++ b/solution.py
@@ -3,6 +3,8 @@
 import jax
 import jax.numpy as jnp
 from jax import lax
+from jax.experimental import pallas as pl
+from jax.experimental.pallas import tpu as pltpu
 from jax.sharding import PartitionSpec as P
 
 HEAD_DIM = 64
@@ -96,7 +98,7 @@
     return state
 
 
-def body(
+def gathered_body(
     tokens,
     first_gain,
     first_shift,
@@ -440,6 +442,463 @@
     )
 
 
+masks = (0, 2, 1, 3)
+tile = 256
+lanes = 256
+
+
+def heads_split(mesh):
+    return mesh.shape["ctx"] == 4 and mesh.shape["dp"] == 8
+
+
+def swap(values, axis, bit):
+    count = lax.axis_size(axis)
+    return lax.ppermute(values, axis, [(i, i ^ bit) for i in range(count)])
+
+
+def gather_rows(values):
+    pair = jnp.concatenate([values, swap(values, "ctx", 2)], axis=0)
+    return jnp.concatenate([pair, swap(pair, "ctx", 1)], axis=0)
+
+
+def scatter_rows(partial):
+    half = partial.shape[0] // 2
+    quarter = half // 2
+    pair = partial[:half] + swap(partial[half:].astype(jnp.bfloat16), "ctx", 1).astype(jnp.float32)
+    return pair[:quarter] + swap(pair[quarter:].astype(jnp.bfloat16), "ctx", 2).astype(jnp.float32)
+
+
+def bit_of(index, bit):
+    return (index // bit) % 2 == 1
+
+
+def dp_gather(values):
+    index = lax.axis_index("dp")
+    values = values[None, None, None]
+    for axis, bit in ((0, 4), (1, 2), (2, 1)):
+        other = swap(values, "dp", bit)
+        upper = bit_of(index, bit)
+        values = jnp.concatenate(
+            [jnp.where(upper, other, values), jnp.where(upper, values, other)], axis=axis
+        )
+    return values.reshape((8,) + values.shape[3:])
+
+
+def dp_scatter(partial):
+    index = lax.axis_index("dp")
+    values = partial.reshape((2, 2, 2) + partial.shape[1:])
+    for axis, bit in ((2, 1), (1, 2), (0, 4)):
+        upper = bit_of(index, bit)
+        low = lax.index_in_dim(values, 0, axis, keepdims=False)
+        high = lax.index_in_dim(values, 1, axis, keepdims=False)
+        sent = jnp.where(upper, low, high).astype(jnp.bfloat16)
+        values = jnp.where(upper, high, low) + swap(sent, "dp", bit).astype(jnp.float32)
+    return values
+
+
+def ctx_parts(values):
+    index = lax.axis_index("ctx")
+    for bit in (2, 1):
+        other = swap(values, "ctx", bit)
+        values = jnp.stack([values, other]) if bit == 2 else jnp.concatenate([values, other])
+    order = [0, 2, 1, 3]
+    out = []
+    for place in range(4):
+        mask = index ^ place
+        spot = (mask % 2) * 2 + mask // 2
+        out.append(lax.dynamic_index_in_dim(values, spot, 0, keepdims=False))
+    return out
+
+
+def to_heads(own):
+    count = own.shape[0] // 4
+    blocks = own.reshape(4, count, own.shape[1])
+    far = swap(jnp.concatenate([blocks[1], blocks[3]], axis=1), "ctx", 2)
+    rows = own.shape[1]
+    near = swap(jnp.concatenate([blocks[2], far[:, rows:]], axis=1), "ctx", 1)
+    return jnp.concatenate([blocks[0], far[:, :rows], near], axis=1)
+
+
+def to_rows(mine):
+    rows = mine.shape[1] // 4
+    part = [mine[:, i * rows : (i + 1) * rows] for i in range(4)]
+    far = swap(jnp.concatenate([part[1], part[3]], axis=1), "ctx", 2)
+    near = swap(jnp.concatenate([part[2], far[:, rows:]], axis=1), "ctx", 1)
+    return jnp.concatenate([part[0], far[:, :rows], near[:, :rows], near[:, rows:]], axis=0)
+
+
+def dot_nt(left, right):
+    return lax.dot_general(left, right, (((1,), (1,)), ((), ())), preferred_element_type=jnp.float32)
+
+
+def dot_nn(left, right):
+    return jnp.dot(left, right, preferred_element_type=jnp.float32)
+
+
+def dot_tn(left, right):
+    return lax.dot_general(left, right, (((0,), (0,)), ((), ())), preferred_element_type=jnp.float32)
+
+
+def place_of(index, spot, rows):
+    return pl.multiple_of((index ^ masks[spot]) * rows, 128)
+
+
+def diagonal():
+    keys = lax.broadcasted_iota(jnp.int32, (tile, tile), 0)
+    queries = lax.broadcasted_iota(jnp.int32, (tile, tile), 1)
+    return keys <= queries
+
+
+def attend_kernel(index_ref, mix_ref, low_ref, full_ref, stats_ref, q_s, k_s, v_s, o_s):
+    total = mix_ref.shape[0]
+    rows = total // 4
+    index = index_ref[0]
+    for spot in range(4):
+        here = pl.ds(spot * rows, rows)
+        there = pl.ds(place_of(index, spot, rows), rows)
+        q_s[there, :] = mix_ref[here, 0:64] * jnp.bfloat16(0.125)
+        k_s[there, :] = mix_ref[here, 64:128]
+        v_s[there, :] = mix_ref[here, 128:192]
+    allowed = diagonal()
+    flipped = v_s[...].astype(jnp.float32).T.astype(jnp.bfloat16)
+    for i in range(total // tile):
+        begin, end = i * tile, (i + 1) * tile
+        queries = q_s[begin:end, :]
+        near = jnp.where(allowed, dot_nt(k_s[begin:end, :], queries), neg_large)
+        top = jnp.max(near, axis=0, keepdims=True)
+        if i > 0:
+            past = dot_nt(k_s[:begin, :], queries)
+            top = jnp.maximum(top, jnp.max(past, axis=0, keepdims=True))
+        near = jnp.exp(near - top)
+        amount = jnp.sum(near, axis=0, keepdims=True)
+        context = dot_nn(flipped[:, begin:end], near.astype(jnp.bfloat16))
+        if i > 0:
+            past = jnp.exp(past - top)
+            amount = amount + jnp.sum(past, axis=0, keepdims=True)
+            context = context + dot_nn(flipped[:, :begin], past.astype(jnp.bfloat16))
+        o_s[:, begin:end] = context / amount
+        stats_ref[0, :, begin:end] = top + jnp.log(amount)
+    for spot in range(4):
+        here = pl.ds(spot * rows, rows)
+        there = pl.ds(place_of(index, spot, rows), rows)
+        block = o_s[:, there]
+        full_ref[:, here] = block
+        low_ref[:, here] = block.astype(jnp.bfloat16)
+
+
+def attend(index, mix):
+    total = mix.shape[0]
+    heads = mix.shape[1] // lanes
+    grid_spec = pltpu.PrefetchScalarGridSpec(
+        num_scalar_prefetch=1,
+        grid=(heads,),
+        in_specs=[pl.BlockSpec((total, lanes), lambda h, s: (0, h))],
+        out_specs=[
+            pl.BlockSpec((HEAD_DIM, total), lambda h, s: (h, 0)),
+            pl.BlockSpec((HEAD_DIM, total), lambda h, s: (h, 0)),
+            pl.BlockSpec((1, 1, total), lambda h, s: (h, 0, 0)),
+        ],
+        scratch_shapes=[pltpu.VMEM((total, HEAD_DIM), jnp.bfloat16)] * 3
+        + [pltpu.VMEM((HEAD_DIM, total), jnp.float32)],
+    )
+    pairs = heads * total * total // 2
+    return pl.pallas_call(
+        attend_kernel,
+        grid_spec=grid_spec,
+        out_shape=[
+            jax.ShapeDtypeStruct((heads * HEAD_DIM, total), jnp.bfloat16),
+            jax.ShapeDtypeStruct((heads * HEAD_DIM, total), jnp.float32),
+            jax.ShapeDtypeStruct((heads, 1, total), jnp.float32),
+        ],
+        compiler_params=pltpu.CompilerParams(vmem_limit_bytes=32 * 1024 * 1024),
+        cost_estimate=pl.CostEstimate(
+            flops=pairs * 4 * 256, bytes_accessed=total * lanes * heads * 4, transcendentals=pairs
+        ),
+        name="attend",
+    )(index, mix)
+
+
+def attend_back_kernel(
+    index_ref, mix_ref, grad_ref, full_ref, stats_ref, out_ref, q_s, k_s, v_s, g_s, d_s, dq_s
+):
+    total = mix_ref.shape[0]
+    rows = total // 4
+    index = index_ref[0]
+    for spot in range(4):
+        here = pl.ds(spot * rows, rows)
+        there = pl.ds(place_of(index, spot, rows), rows)
+        q_s[there, :] = mix_ref[here, 0:64] * jnp.bfloat16(0.125)
+        k_s[there, :] = mix_ref[here, 64:128]
+        v_s[there, :] = mix_ref[here, 128:192]
+        block = grad_ref[:, here]
+        g_s[:, there] = block
+        d_s[:, there] = jnp.sum(block.astype(jnp.float32) * full_ref[:, here], axis=0, keepdims=True)
+    allowed = diagonal()
+    turned = g_s[...].astype(jnp.float32).T.astype(jnp.bfloat16)
+    flipped = k_s[...].astype(jnp.float32).T.astype(jnp.bfloat16)
+    count = total // tile
+    dkv = []
+    for j in range(count):
+        begin, end = j * tile, (j + 1) * tile
+        keys, values = k_s[begin:end, :], v_s[begin:end, :]
+        probs = jnp.exp(dot_nt(keys, q_s[begin:, :]) - stats_ref[0, :, begin:])
+        near = jnp.where(allowed, probs[:, :tile], 0.0)
+        probs = near if j == count - 1 else jnp.concatenate([near, probs[:, tile:]], axis=1)
+        scores = (probs * (dot_nn(values, g_s[:, begin:]) - d_s[:, begin:])).astype(jnp.bfloat16)
+        grad_value = dot_nn(probs.astype(jnp.bfloat16), turned[begin:, :])
+        grad_key = dot_nn(scores, q_s[begin:, :])
+        update = dot_nn(flipped[:, begin:end], scores)
+        if j == 0:
+            dq_s[...] = update
+        else:
+            dq_s[:, begin:] = dq_s[:, begin:] + update
+        k_s[begin:end, :] = grad_key.astype(jnp.bfloat16)
+        v_s[begin:end, :] = grad_value.astype(jnp.bfloat16)
+    q_s[...] = (dq_s[...] * 0.125).T.astype(jnp.bfloat16)
+    for spot in range(4):
+        here = pl.ds(spot * rows, rows)
+        there = pl.ds(place_of(index, spot, rows), rows)
+        out_ref[here, 0:64] = q_s[there, :]
+        out_ref[here, 64:128] = k_s[there, :]
+        out_ref[here, 128:192] = v_s[there, :]
+        out_ref[here, 192:256] = jnp.zeros((rows, 64), jnp.bfloat16)
+
+
+def attend_back(index, mix, grad, full, stats):
+    total = mix.shape[0]
+    heads = mix.shape[1] // lanes
+    grid_spec = pltpu.PrefetchScalarGridSpec(
+        num_scalar_prefetch=1,
+        grid=(heads,),
+        in_specs=[
+            pl.BlockSpec((total, lanes), lambda h, s: (0, h)),
+            pl.BlockSpec((HEAD_DIM, total), lambda h, s: (h, 0)),
+            pl.BlockSpec((HEAD_DIM, total), lambda h, s: (h, 0)),
+            pl.BlockSpec((1, 1, total), lambda h, s: (h, 0, 0)),
+        ],
+        out_specs=pl.BlockSpec((total, lanes), lambda h, s: (0, h)),
+        scratch_shapes=[pltpu.VMEM((total, HEAD_DIM), jnp.bfloat16)] * 3
+        + [
+            pltpu.VMEM((HEAD_DIM, total), jnp.bfloat16),
+            pltpu.VMEM((1, total), jnp.float32),
+            pltpu.VMEM((HEAD_DIM, total), jnp.float32),
+        ],
+    )
+    pairs = heads * total * total // 2
+    return pl.pallas_call(
+        attend_back_kernel,
+        grid_spec=grid_spec,
+        out_shape=jax.ShapeDtypeStruct(mix.shape, jnp.bfloat16),
+        compiler_params=pltpu.CompilerParams(vmem_limit_bytes=40 * 1024 * 1024),
+        cost_estimate=pl.CostEstimate(
+            flops=pairs * 10 * 256, bytes_accessed=total * lanes * heads * 8, transcendentals=pairs
+        ),
+        name="attend_back",
+    )(index, mix, grad, full, stats)
+
+
+def normalized(values):
+    center = values - jnp.mean(values, axis=-1, keepdims=True)
+    spread = jnp.mean(center * center, axis=-1, keepdims=True)
+    scale = lax.rsqrt(spread + epsilon)
+    return center * scale, scale
+
+
+def norm_pull(unit, scale, gain, upstream):
+    scaled = upstream * gain
+    return scale * (
+        scaled
+        - jnp.mean(scaled, axis=-1, keepdims=True)
+        - unit * jnp.mean(scaled * unit, axis=-1, keepdims=True)
+    )
+
+
+def split_body(
+    tokens,
+    first_gain,
+    first_shift,
+    in_weight,
+    in_bias,
+    out_weight,
+    out_bias,
+    second_gain,
+    second_shift,
+    up_weight,
+    up_bias,
+    down_weight,
+    down_bias,
+    cotangent,
+):
+    low, wide = jnp.bfloat16, jnp.float32
+    width = tokens.shape[1]
+    n_dp = lax.axis_size("dp")
+    shard = width // n_dp
+    ctx = lax.axis_index("ctx")
+    heads = width // HEAD_DIM // 4
+    own = heads * HEAD_DIM
+    index = ctx.astype(jnp.int32).reshape(1)
+
+    in_own = lax.dynamic_index_in_dim(
+        in_weight.reshape(shard, 3, 4, heads, HEAD_DIM), ctx, 2, keepdims=False
+    )
+    in_own = in_own.transpose(0, 2, 1, 3).reshape(shard, 3 * own)
+    vectors = jnp.concatenate(
+        [first_gain, first_shift, in_bias[0], in_bias[1], out_bias, second_gain, second_shift]
+        + [down_bias, up_bias]
+    ).reshape(2, 3 * own)
+    gathered = dp_gather(jnp.concatenate([in_own, vectors], axis=0))
+    in_full = gathered[:, :shard].reshape(width, heads, 3 * HEAD_DIM)
+    in_full = jnp.pad(in_full, ((0, 0), (0, 0), (0, lanes - 3 * HEAD_DIM))).reshape(
+        width, heads * lanes
+    )
+    vectors = gathered[:, shard:].reshape(n_dp, 12, shard).astype(wide)
+    gain_one, shift_one, query_bias, value_bias, out_bias, gain_two, shift_two, down_bias = [
+        vectors[:, i].reshape(width) for i in range(8)
+    ]
+    up_bias = lax.dynamic_index_in_dim(vectors[:, 8:], ctx, 1, keepdims=False).reshape(width)
+    bias_full = jnp.stack(
+        [
+            lax.dynamic_slice_in_dim(query_bias, ctx * own, own).reshape(heads, HEAD_DIM),
+            jnp.zeros((heads, HEAD_DIM), wide),
+            lax.dynamic_slice_in_dim(value_bias, ctx * own, own).reshape(heads, HEAD_DIM),
+            jnp.zeros((heads, HEAD_DIM), wide),
+        ],
+        axis=1,
+    ).reshape(heads * lanes)
+
+    up_own = lax.dynamic_index_in_dim(
+        up_weight.reshape(shard, n_dp, 4, shard), ctx, 2, keepdims=False
+    ).reshape(shard, width)
+    down_own = lax.dynamic_slice_in_dim(down_weight, ctx * shard, shard, 0)
+    up_full = dp_gather(up_own).reshape(width, width)
+    down_full = dp_gather(down_own).reshape(width, width)
+    out_full = lax.all_gather(out_weight, "dp", axis=0, tiled=True)
+    out_rel = jnp.concatenate(
+        [lax.dynamic_slice_in_dim(out_full, (ctx ^ mask) * own, own, 0) for mask in masks], axis=0
+    )
+
+    unit_one, scale_one = normalized(gather_rows(tokens).astype(wide))
+    first_low = (unit_one * gain_one + shift_one).astype(low)
+    mix = (dot_nn(first_low, in_full) + bias_full).astype(low)
+    context_mine, context_full, stats = attend(index, mix)
+    context_low = to_rows(context_mine)
+    inputs = tokens.astype(wide)
+    residual = inputs + dot_tn(context_low, out_rel) + out_bias
+
+    unit_two, scale_two = normalized(residual)
+    second_low = gather_rows((unit_two * gain_two + shift_two).astype(low))
+    upstream_all = gather_rows(cotangent)
+    hidden = dot_nn(second_low, up_full) + up_bias
+    root = math.sqrt(2.0 / math.pi)
+    square = hidden * hidden
+    bend = jnp.tanh(root * hidden * (1.0 + 0.044715 * square))
+    active_low = (0.5 * hidden * (1.0 + bend)).astype(low)
+    slope = 0.5 * (1.0 + bend) + 0.5 * hidden * (1.0 - bend * bend) * (
+        root * (1.0 + 3 * 0.044715 * square)
+    )
+    grad_hidden = (slope * dot_nt(upstream_all, down_full)).astype(low)
+    grad_second = scatter_rows(dot_nt(grad_hidden, up_full))
+    branch = scatter_rows(dot_nn(active_low, down_full))
+    layer_out = (residual + branch + down_bias).astype(low)
+
+    down_weight_grad = dot_tn(active_low, upstream_all)
+    up_weight_grad = dot_tn(second_low, grad_hidden)
+    up_bias_grad = jnp.sum(grad_hidden.astype(wide), axis=0)
+    upstream = cotangent.astype(wide)
+    down_bias_grad = jnp.sum(upstream, axis=0)
+    second_gain_grad = jnp.sum(grad_second * unit_two, axis=0)
+    second_shift_grad = jnp.sum(grad_second, axis=0)
+    grad_residual = upstream + norm_pull(unit_two, scale_two, gain_two, grad_second)
+    grad_attn = grad_residual.astype(low)
+    out_bias_grad = jnp.sum(grad_attn.astype(wide), axis=0)
+    grad_context = to_heads(dot_nt(out_rel, grad_attn).astype(low))
+    out_weight_rel = dot_nn(context_low, grad_attn).reshape(4, own, width)
+    out_weight_grad = jnp.concatenate(
+        [
+            lax.dynamic_index_in_dim(
+                out_weight_rel,
+                ((ctx ^ place) % 2) * 2 + (ctx ^ place) // 2,
+                0,
+                keepdims=False,
+            )
+            for place in range(4)
+        ],
+        axis=0,
+    )
+
+    grad_mix = attend_back(index, mix, grad_context, context_full, stats)
+    in_weight_grad = dot_tn(first_low, grad_mix).reshape(width, heads, lanes)
+    in_weight_grad = in_weight_grad[:, :, : 3 * HEAD_DIM].reshape(n_dp, shard, 3 * own)
+    sums = jnp.sum(grad_mix.astype(wide), axis=0).reshape(heads, 4, HEAD_DIM)
+    own_bias = jnp.zeros((2, 4, own), wide)
+    own_bias = lax.dynamic_update_slice(
+        own_bias, jnp.stack([sums[:, 0].reshape(1, own), sums[:, 2].reshape(1, own)]), (0, ctx, 0)
+    ).reshape(2, width)
+    grad_first_part = dot_nt(grad_mix, in_full)
+    first_gain_grad = jnp.sum(grad_first_part * unit_one, axis=0)
+    first_shift_grad = jnp.sum(grad_first_part, axis=0)
+    grad_first = scatter_rows(grad_first_part)
+    rows = tokens.shape[0]
+    tokens_grad = (
+        grad_residual + norm_pull(unit_one[:rows], scale_one[:rows], gain_one, grad_first)
+    ).astype(low)
+
+    def rows_of(parts, columns):
+        flat = jnp.concatenate([part.reshape(n_dp, shard) for part in parts], axis=1)
+        return jnp.pad(flat, ((0, 0), (0, columns - flat.shape[1])))[:, None]
+
+    late = [first_gain_grad, first_shift_grad, own_bias[0], own_bias[1]]
+    early = [up_bias_grad, down_bias_grad, second_gain_grad, second_shift_grad, out_bias_grad]
+    down_mine = dp_scatter(down_weight_grad.reshape(n_dp, shard, width))
+    up_mine = dp_scatter(up_weight_grad.reshape(n_dp, shard, width))
+    out_mine = dp_scatter(
+        jnp.concatenate([out_weight_grad.reshape(n_dp, shard, width), rows_of(early, width)], 1)
+    )
+    in_mine = dp_scatter(jnp.concatenate([in_weight_grad, rows_of(late, 3 * own)], 1))
+    first = ctx_parts(jnp.concatenate([down_mine, up_mine, out_mine]).astype(low))
+    last = ctx_parts(in_mine.astype(low))
+    first = [part.astype(wide) for part in first]
+    last = [part.astype(wide) for part in last]
+    down_weight_grad = jnp.concatenate([part[:shard] for part in first], axis=0)
+    up_weight_grad = jnp.stack(
+        [part[shard : 2 * shard].reshape(shard, n_dp, shard) for part in first], axis=2
+    ).reshape(shard, 4 * width)
+    summed = first[0][2 * shard :] + first[1][2 * shard :] + first[2][2 * shard :]
+    summed = summed + first[3][2 * shard :]
+    out_weight_grad = summed[:shard]
+    up_bias_grad = jnp.concatenate([part[3 * shard, :shard] for part in first])
+    down_bias_grad, second_gain_grad, second_shift_grad, out_bias_grad = [
+        summed[shard, i * shard : (i + 1) * shard] for i in range(1, 5)
+    ]
+    in_weight_grad = jnp.stack(
+        [
+            part[:shard].reshape(shard, heads, 3, HEAD_DIM).transpose(0, 2, 1, 3)
+            for part in last
+        ],
+        axis=2,
+    ).reshape(shard, 3 * width)
+    summed = last[0][shard] + last[1][shard] + last[2][shard] + last[3][shard]
+    first_gain_grad = summed[:shard]
+    first_shift_grad = summed[shard : 2 * shard]
+    in_bias_grad = summed[2 * shard : 4 * shard].reshape(2, shard)
+    return (
+        layer_out,
+        tokens_grad,
+        first_gain_grad,
+        first_shift_grad,
+        in_weight_grad,
+        in_bias_grad,
+        out_weight_grad,
+        out_bias_grad,
+        second_gain_grad,
+        second_shift_grad,
+        up_weight_grad,
+        up_bias_grad,
+        down_weight_grad,
+        down_bias_grad,
+    )
+
+
 def solution(mesh):
     in_specs = (
         P(("dp", "ctx"), None),
@@ -473,4 +932,5 @@
         P("dp", None),
         P("dp"),
     )
-    return jax.shard_map(body, mesh=mesh, in_specs=in_specs, out_specs=out_specs, check_vma=False)
+    chosen = split_body if heads_split(mesh) else gathered_body
+    return jax.shard_map(chosen, mesh=mesh, in_specs=in_specs, out_specs=out_specs, check_vma=False)

time: 958 us -> 393 us (0.41)
  waiting for transfers between devices: 597 us -> 105 us
  blocking collectives: 127 us -> 0 us
  matrix products: 101 us -> 39.8 us
  starting transfers between devices: 0.48 us -> 40.5 us
  local copies, waits for them, and re-layouts: 60.2 us -> 96 us
  other arithmetic: 36.6 us -> 65.6 us
  Pallas kernels: 0 us -> 25 us
  loops' own time: 12.1 us -> 0 us
    reduce_scatter x5 -> x0, waiting for transfers between devices: 335 us -> none  [the longest x1 99.1 us: body(): lax.psum_scatter(down_weight_grad.astype(jnp.bfloat16), 'dp', scatter_dim...]
    all_gather x6 -> x1, waiting for transfers between devices: 165 us -> 0.01 us  [split_body(): out_full = lax.all_gather(out_weight, 'dp', axis=0, tiled=True)]
    ppermute x0 -> x41, waiting for transfers between devices: none -> 105 us  [swap(): return lax.ppermute(values, axis, [(i, i ^ bit) for i in range(count)])]
    unnamed x2 -> x0, blocking collectives: 77.7 us -> none
    dot_general x19 -> x12, matrix products: 101 us -> 39.8 us  [the longest x4 16.6 us: dot_nt(): lax.dot_general(left, right, (((1,), (1,)), ((), ())), preferred_element_...]
    unnamed x14 -> x1, waiting for transfers between devices: 60.4 us -> 0.02 us
    all_gather x2 -> x0, blocking collectives: 43.1 us -> none  [the longest x1 26.5 us: body(): lax.all_gather(up_bias, 'dp', axis=0, tiled=True)]
    ppermute x0 -> x41, starting transfers between devices: none -> 40.5 us  [swap(): return lax.ppermute(values, axis, [(i, i ^ bit) for i in range(count)])]
  transfers between devices with their start and end apart: 13 -> 42, of which waited for: 13 -> 18; matrix products, arithmetic and copies ran while one was open for 14% -> 36% of each run, Pallas kernels for 0% -> 6%
where the time goes in v1:
time: 393 us; the launch traced here: 388 us
  waiting for transfers between devices  105 us (27%)
  local copies, waits for them, and re-layouts  96 us (24%)
  other arithmetic  65.6 us (17%)
  starting transfers between devices  40.5 us (10%)
  matrix products  39.8 us (10%)
  Pallas kernels  25 us (6%)
  between operations  16.2 us (4%)
    ppermute x41, waiting for transfers between devices, swap(): return lax.ppermute(values, axis, [(i, i ^ bit) for i in range(count)])  105 us
    ppermute x41, starting transfers between devices, swap(): return lax.ppermute(values, axis, [(i, i ^ bit) for i in range(count)])  40.5 us
    dot_general x4, matrix products, dot_nt(): lax.dot_general(left, right, (((1,), (1,)), ((), ())), preferred_element_...  16.6 us
    unnamed x178, local copies, waits for them, and re-layouts  15.8 us
    pallas_call x1, Pallas kernels, attend_back(): pl.pallas_call(attend_back_kernel, grid_spec=grid_spec, out_shape=jax.Sha...  14.8 us
    dot_general x4, matrix products, dot_tn(): lax.dot_general(left, right, (((0,), (0,)), ((), ())), preferred_element_...  12.1 us
    dot_general x4, matrix products, dot_nn(): return jnp.dot(left, right, preferred_element_type=jnp.float32)  11.1 us
    concatenate x4, local copies, waits for them, and re-layouts, split_body(): jnp.concatenate([in_weight_grad, rows_of(late, 3 * own)], 1)  10.8 us
  transfers between devices with their start and end apart: 42, of which 18 were waited for; matrix products, arithmetic and copies ran while one was open for 36% of the time, Pallas kernels for 6%

profile of v1, /device:TPU:0, one launch (start us, length us, event | category | flops | bytes accessed | tf_op | source)
XLA Modules:
  0.0 388.5 jit_solution(2053114082036867405)
XLA Ops:
  9.4 4.8 %concatenate.136 = bf16[1152]{0:T(1024)(128)(2,1)S(1)} concatenate(bf16[96]{0:T(256)(128)(2,1)} %param.15, bf16[96]{0:T(256)(128)(2,1)} %param.16, bf16[96]{0:T(256)(128)(2,1)S(1)} %get-tuple-element.186, bf16[96]{0:T(256)(128)(2,1)S(1)} %get-tuple-element.185, bf16[96]{0:T(256)(128)(2,1)} %param.20, bf16[96]{0:T(256)(128)(2,1)} %param.21, bf16[96]{0:T(256)(128)(2,1)} %param.22, ...), dimensions={0} | concatenate | bytes 4608 | tf_op jit(solution)/shard_map/concatenate | solution.py:745
  14.6 4.1 %collective-permute-start.2 = (bf16[1,1,1,98,576]{3,4,2,1,0:T(8,128)(2,1)S(1)}, bf16[1,1,1,98,576]{3,4,2,1,0:T(8,128)(2,1)S(1)}, u32[]{:S(2)}, u32[]{:S(2)}) collective-permute-start(bf16[1,1,1,98,576]{3,4,2,1,0:T(8,128)(2,1)S(1)} %maximum_bitcast_fusion), channel_id=1, source_target_pairs={{0,16},{4,20},{8,24},{12,28},{16,0},{20,4},{24,8},{28,12},{1,17},{... | collective-permute-start | bytes 338696 | tf_op jit(solution)/shard_map/ppermute | solution.py:456
  18.7 7.0 %collective-permute-done.2 = bf16[1,1,1,98,576]{3,4,2,1,0:T(8,128)(2,1)S(1)} collective-permute-done((bf16[1,1,1,98,576]{3,4,2,1,0:T(8,128)(2,1)S(1)}, bf16[1,1,1,98,576]{3,4,2,1,0:T(8,128)(2,1)S(1)}, u32[]{:S(2)}, u32[]{:S(2)}) %collective-permute-start.2) | collective-permute-done | bytes 112928 | tf_op jit(solution)/shard_map/ppermute | solution.py:456
  30.5 3.4 collective-permute-start.9
  38.6 4.3 %collective-permute-done = bf16[384,768]{1,0:T(8,128)(2,1)S(1)} collective-permute-done((bf16[384,768]{1,0:T(8,128)(2,1)S(1)}, bf16[384,768]{1,0:T(8,128)(2,1)S(1)}, u32[]{:S(2)}, u32[]{:S(2)}) %collective-permute-start) | collective-permute-done | bytes 589856 | tf_op jit(solution)/shard_map/ppermute | solution.py:456
  65.1 3.7 add_convert_fusion.mix_ref
  68.8 10.3 %attend.1 = (bf16[192,1536]{1,0:T(8,128)(2,1)S(1)}, f32[192,1536]{1,0:T(8,128)S(1)}, f32[3,1,1536]{2,1,0:T(1,128)S(1)}) custom-call(s32[1]{0:T(128)} %bitcast.index_ref, bf16[1536,768]{1,0:T(8,128)(2,1)S(1)} %add_convert_fusion.mix_ref), custom_call_target="tpu_custom_call" | custom-call | flops 3623878656 | bytes 4718592 | tf_op jit(solution)/shard_map/attend/pallas_call | solution.py:605
  83.7 4.5 %collective-permute-done.5 = bf16[192,768]{1,0:T(8,128)(2,1)S(1)} collective-permute-done((bf16[192,768]{1,0:T(8,128)(2,1)S(1)}, bf16[192,768]{1,0:T(8,128)(2,1)S(1)}, u32[]{:S(2)}, u32[]{:S(2)}) %collective-permute-start.5) | collective-permute-done | bytes 294944 | tf_op jit(solution)/shard_map/ppermute | solution.py:456
  103.7 7.7 %collective-permute-done.7 = bf16[384,768]{1,0:T(8,128)(2,1)S(1)} collective-permute-done((bf16[384,768]{1,0:T(8,128)(2,1)S(1)}, bf16[384,768]{1,0:T(8,128)(2,1)S(1)}, u32[]{:S(2)}, u32[]{:S(2)}) %collective-permute-start.7) | collective-permute-done | bytes 589856 | tf_op jit(solution)/shard_map/ppermute | solution.py:456
  120.1 5.8 %collective-permute-done.14 = bf16[2,2,1,96,768]{4,3,2,1,0:T(8,128)(2,1)} collective-permute-done((bf16[2,2,1,96,768]{4,3,2,1,0:T(8,128)(2,1)}, bf16[2,2,1,96,768]{4,3,2,1,0:T(8,128)(2,1)}, u32[]{:S(2)}, u32[]{:S(2)}) %collective-permute-start.14) | collective-permute-done | bytes 589856 | tf_op jit(solution)/shard_map/ppermute | solution.py:456
  128.7 3.3 fusion.13
  134.8 4.9 %convert_reduce_fusion.1 = (f32[768]{0:T(1024)}, bf16[1536,768]{1,0:T(8,128)(2,1)S(1)}) fusion(bf16[1536,768]{1,0:T(8,128)(2,1)S(1)} %constant_dynamic-update-slice_fusion, bf16[768,768]{1,0:T(8,128)(2,1)S(1)} %bitcast.264, f32[1536,768]{1,0:T(8,128)S(1)} %fusion.13, f32[768]{0:T(1024)S(1)} %copy-done.79), kind=kOutput, calls=%fused_computation.5 | convolution fusion | flops 1836711168 | bytes 10622976 | tf_op jit(solution)/shard_map/dot_general | solution.py:531
  139.7 3.1 fusion.51
  146.0 3.4 fusion.12
  164.4 8.7 %collective-permute-done.33 = bf16[2,2,96,768]{3,2,1,0:T(8,128)(2,1)} collective-permute-done((bf16[2,2,96,768]{3,2,1,0:T(8,128)(2,1)}, bf16[2,2,96,768]{3,2,1,0:T(8,128)(2,1)}, u32[]{:S(2)}, u32[]{:S(2)}) %collective-permute-start.33) | collective-permute-done | bytes 589856 | tf_op jit(solution)/shard_map/ppermute | solution.py:456
  175.6 4.2 %collective-permute-start.32 = (bf16[96,768]{1,0:T(8,128)(2,1)S(1)}, bf16[96,768]{1,0:T(8,128)(2,1)S(1)}, u32[]{:S(2)}, u32[]{:S(2)}) collective-permute-start(bf16[96,768]{1,0:T(8,128)(2,1)S(1)} %fusion.34), channel_id=1, source_target_pairs={{0,16},{4,20},{8,24},{12,28},{16,0},{20,4},{24,8},{28,12},{1,17},{... | collective-permute-start | bytes 442376 | tf_op jit(solution)/shard_map/ppermute | solution.py:456
  179.8 5.4 %collective-permute-done.34 = bf16[2,96,768]{2,1,0:T(8,128)(2,1)S(1)} collective-permute-done((bf16[2,96,768]{2,1,0:T(8,128)(2,1)S(1)}, bf16[2,96,768]{2,1,0:T(8,128)(2,1)S(1)}, u32[]{:S(2)}, u32[]{:S(2)}) %collective-permute-start.34) | collective-permute-done | bytes 294944 | tf_op jit(solution)/shard_map/ppermute | solution.py:456
  194.9 11.7 %collective-permute-done.20 = bf16[384,768]{1,0:T(8,128)(2,1)S(1)} collective-permute-done((bf16[384,768]{1,0:T(8,128)(2,1)S(1)}, bf16[384,768]{1,0:T(8,128)(2,1)S(1)}, u32[]{:S(2)}, u32[]{:S(2)}) %collective-permute-start.20) | collective-permute-done | bytes 589856 | tf_op jit(solution)/shard_map/ppermute | solution.py:456
  207.7 9.0 %collective-permute-done.16 = bf16[384,768]{1,0:T(8,128)(2,1)S(1)} collective-permute-done((bf16[384,768]{1,0:T(8,128)(2,1)S(1)}, bf16[384,768]{1,0:T(8,128)(2,1)S(1)}, u32[]{:S(2)}, u32[]{:S(2)}) %collective-permute-start.16) | collective-permute-done | bytes 589856 | tf_op jit(solution)/shard_map/ppermute | solution.py:456
  216.7 3.3 convert_reduce_fusion.4
  234.2 14.8 %attend_back.1 = bf16[1536,768]{1,0:T(8,128)(2,1)S(1)} custom-call(s32[1]{0:T(128)} %bitcast.index_ref, bf16[1536,768]{1,0:T(8,128)(2,1)S(1)} %copy-done.1, bf16[192,1536]{1,0:T(8,128)(2,1)S(1)} %pad_maximum_fusion.23.grad_ref, f32[192,1536]{1,0:T(8,128)S(1)} %get-tuple-element.18.full_ref, f32[3,1,1536]{2,1,0:T(1,128)S(1)} %copy-done.3), custom_call_target="tpu_custom_call" | custom-call | flops 9059696640 | bytes 9437184 | tf_op jit(solution)/shard_map/attend_back/pallas_call | solution.py:688
  257.0 8.9 %multiply_reduce_fusion = (f32[768]{0:T(1024)}, f32[768]{0:T(1024)}, f32[1536,768]{1,0:T(8,128)}, f32[1536,768]{1,0:T(8,128)}) fusion(f32[1536]{0:T(1024)} %copy-done.77, f32[1536]{0:T(1024)S(1)} %copy-done.69, bf16[768,768]{1,0:T(8,128)(2,1)} %collective-permute-done.1, bf16[384,768]{1,0:T(8,128)(2,1)S(1)} %copy-done.16, ...), kind=kOutput, calls=%fused_computation.7 | convolution fusion | flops 1824913920 | bytes 15353856 | tf_op jit(solution)/shard_map/dot_general | solution.py:531
  268.6 3.8 fusion.17
  277.2 4.9 %concatenate.158 = f32[2,2,2,96,576]{3,2,1,0,4:T(2,128)} reshape(f32[768,3,192]{0,2,1:T(8,128)S(1)} %slice.505) | data formatting | bytes 3538944 | tf_op jit(solution)/shard_map/concatenate | solution.py:857
  282.1 5.8 %copy.220 = f32[2,2,2,96,576]{4,1,3,2,0:T(2,128)S(1)} copy(f32[2,2,2,96,576]{3,2,1,0,4:T(2,128)} %concatenate.158) | data formatting | bytes 3538944 | tf_op jit(solution)/shard_map/concatenate | solution.py:857
  294.5 7.9 %collective-permute-done.25 = bf16[2,2,97,576]{3,1,2,0:T(2,128)(2,1)S(1)} collective-permute-done((bf16[2,2,97,576]{3,1,2,0:T(2,128)(2,1)S(1)}, bf16[2,2,97,576]{3,1,2,0:T(2,128)(2,1)S(1)}, u32[]{:S(2)}, u32[]{:S(2)}) %collective-permute-start.25) | collective-permute-done | bytes 447008 | tf_op jit(solution)/shard_map/ppermute | solution.py:456
  305.9 6.3 %collective-permute-done.26 = bf16[2,97,576]{2,1,0:T(8,128)(2,1)S(1)} collective-permute-done((bf16[2,97,576]{2,1,0:T(8,128)(2,1)S(1)}, bf16[2,97,576]{2,1,0:T(8,128)(2,1)S(1)}, u32[]{:S(2)}, u32[]{:S(2)}) %collective-permute-start.26) | collective-permute-done | bytes 223520 | tf_op jit(solution)/shard_map/ppermute | solution.py:456
  313.9 6.0 %collective-permute-done.27 = bf16[97,576]{1,0:T(8,128)(2,1)S(1)} collective-permute-done((bf16[97,576]{1,0:T(8,128)(2,1)S(1)}, bf16[97,576]{1,0:T(8,128)(2,1)S(1)}, u32[]{:S(2)}, u32[]{:S(2)}) %collective-permute-start.27) | collective-permute-done | bytes 111776 | tf_op jit(solution)/shard_map/ppermute | solution.py:456
  321.0 5.0 %collective-permute-done.28 = bf16[97,576]{1,0:T(8,128)(2,1)S(1)} collective-permute-done((bf16[97,576]{1,0:T(8,128)(2,1)S(1)}, bf16[97,576]{1,0:T(8,128)(2,1)S(1)}, u32[]{:S(2)}, u32[]{:S(2)}) %collective-permute-start.28) | collective-permute-done | bytes 111776 | tf_op jit(solution)/shard_map/ppermute | solution.py:456
  343.4 8.6 %collective-permute-done.24 = bf16[384,768]{1,0:T(8,128)(2,1)} collective-permute-done((bf16[384,768]{1,0:T(8,128)(2,1)}, bf16[384,768]{1,0:T(8,128)(2,1)}, u32[]{:S(2)}, u32[]{:S(2)}) %collective-permute-start.24) | collective-permute-done | bytes 589856 | tf_op jit(solution)/shard_map/ppermute | solution.py:456
  356.6 4.0 %pad_maximum_fusion.3 = bf16[4,289,768]{2,0,1:T(4,128)(2,1)S(1)} fusion(bf16[2,289,768]{2,0,1:T(2,128)(2,1)} %collective-permute-done.40, bf16[1,289,768]{2,0,1:T(2,128)(2,1)S(1)} %copy-done.19, bf16[1,289,768]{2,0,1:T(2,128)(2,1)S(1)} %copy-done.18), kind=kLoop, calls=%fused_computation.26 | loop fusion | flops 5326848 | bytes 3551232 | tf_op jit(solution)/shard_map/concatenate | solution.py:503
  360.6 3.8 dynamic-slice_convert_fusion
  (450 shorter events, 179.8 us)
Async XLA Ops:
  7.2 84.3 %all-gather.2.cloned.1.call-start = ((), (), s32[]{:S(2)}) async-start(), calls=%async_computation | async-start | bytes 1327104 | tf_op jit(solution)/shard_map/all_gather | solution.py:775
  14.6 11.1 %collective-permute-start.2 = (bf16[1,1,1,98,576]{3,4,2,1,0:T(8,128)(2,1)S(1)}, bf16[1,1,1,98,576]{3,4,2,1,0:T(8,128)(2,1)S(1)}, u32[]{:S(2)}, u32[]{:S(2)}) collective-permute-start(bf16[1,1,1,98,576]{3,4,2,1,0:T(8,128)(2,1)S(1)} %maximum_bitcast_fusion), channel_id=1, source_target_pairs={{0,16},{4,20},{8,24},{12,28},{16,0},{20,4},{24,8},{28,12},{1,17},{... | collective-permute-start | bytes 338696 | tf_op jit(solution)/shard_map/ppermute | solution.py:456
  26.8 16.2 %collective-permute-start = (bf16[384,768]{1,0:T(8,128)(2,1)S(1)}, bf16[384,768]{1,0:T(8,128)(2,1)S(1)}, u32[]{:S(2)}, u32[]{:S(2)}) collective-permute-start(bf16[384,768]{1,0:T(8,128)(2,1)S(1)} %copy-done.11), channel_id=1, source_target_pairs={{0,2},{1,3},{2,0},{3,1},{4,6},{5,7},{6,4},{7,5},{8,10},{9,11},{10,... | collective-permute-start | bytes 1769480 | tf_op jit(solution)/shard_map/ppermute | solution.py:456
  30.5 16.0 %collective-permute-start.9 = (bf16[1,1,1,96,768]{4,3,2,1,0:T(8,128)(2,1)S(1)}, bf16[1,1,1,96,768]{4,3,2,1,0:T(8,128)(2,1)}, u32[]{:S(2)}, u32[]{:S(2)}) collective-permute-start(bf16[1,1,1,96,768]{4,3,2,1,0:T(8,128)(2,1)S(1)} %broadcast_in_dim_reshape.2), channel_id=1, source_target_pairs={{0,16},{4,20},{8,24},{12,28},{16,0},{20,4},{24,8},{28,12},{1,17},{... | collective-permute-start | bytes 442376 | tf_op jit(solution)/shard_map/ppermute | solution.py:456
  33.9 67.5 %collective-permute-start.17 = (bf16[384,768]{1,0:T(8,128)(2,1)}, bf16[384,768]{1,0:T(8,128)(2,1)}, u32[]{:S(2)}, u32[]{:S(2)}) collective-permute-start(bf16[384,768]{1,0:T(8,128)(2,1)} %param.27), channel_id=1, source_target_pairs={{0,2},{1,3},{2,0},{3,1},{4,6},{5,7},{6,4},{7,5},{8,10},{9,11},{10,... | collective-permute-start | bytes 1769480 | tf_op jit(solution)/shard_map/ppermute | solution.py:456
  36.0 45.4 %collective-permute-start.12 = (bf16[1,1,1,96,768]{4,3,2,1,0:T(8,128)(2,1)}, bf16[1,1,1,96,768]{4,3,2,1,0:T(8,128)(2,1)}, u32[]{:S(2)}, u32[]{:S(2)}) collective-permute-start(bf16[1,1,1,96,768]{4,3,2,1,0:T(8,128)(2,1)} %dynamic-slice_bitcast_fusion.4), channel_id=1, source_target_pairs={{0,16},{4,20},{8,24},{12,28},{16,0},{20,4},{24,8},{28,12},{1,17},{... | collective-permute-start | bytes 442376 | tf_op jit(solution)/shard_map/ppermute | solution.py:456
  37.1 13.9 %collective-permute-start.4 = (bf16[2,2,1,98,576]{4,1,3,2,0:T(2,128)(2,1)S(1)}, bf16[2,2,1,98,576]{4,1,3,2,0:T(2,128)(2,1)S(1)}, u32[]{:S(2)}, u32[]{:S(2)}) collective-permute-start(bf16[2,2,1,98,576]{4,1,3,2,0:T(2,128)(2,1)S(1)} %copy.214), channel_id=1, source_target_pairs={{0,4},{4,0},{8,12},{12,8},{16,20},{20,16},{24,28},{28,24},{1,5},{5... | collective-permute-start | bytes 1354760 | tf_op jit(solution)/shard_map/ppermute | solution.py:456
  44.2 15.8 %collective-permute-start.1 = (bf16[768,768]{1,0:T(8,128)(2,1)}, bf16[768,768]{1,0:T(8,128)(2,1)}, u32[]{:S(2)}, u32[]{:S(2)}) collective-permute-start(bf16[768,768]{1,0:T(8,128)(2,1)} %pad_maximum_fusion.6), channel_id=1, source_target_pairs={{0,1},{1,0},{2,3},{3,2},{4,5},{5,4},{6,7},{7,6},{8,9},{9,8},{10,11... | collective-permute-start | bytes 3538952 | tf_op jit(solution)/shard_map/ppermute | solution.py:456
  48.2 41.4 %collective-permute-start.10 = (bf16[2,1,1,96,768]{4,3,2,1,0:T(8,128)(2,1)}, bf16[2,1,1,96,768]{4,3,2,1,0:T(8,128)(2,1)}, u32[]{:S(2)}, u32[]{:S(2)}) collective-permute-start(bf16[2,1,1,96,768]{4,3,2,1,0:T(8,128)(2,1)} %pad_maximum_fusion.30), channel_id=1, source_target_pairs={{0,8},{4,12},{8,0},{12,4},{16,24},{20,28},{24,16},{28,20},{1,9},{5... | collective-permute-start | bytes 884744 | tf_op jit(solution)/shard_map/ppermute | solution.py:456
  83.3 14.6 %collective-permute-start.13 = (bf16[2,1,1,96,768]{4,3,2,1,0:T(8,128)(2,1)}, bf16[2,1,1,96,768]{4,3,2,1,0:T(8,128)(2,1)}, u32[]{:S(2)}, u32[]{:S(2)}) collective-permute-start(bf16[2,1,1,96,768]{4,3,2,1,0:T(8,128)(2,1)} %pad_maximum_fusion.31), channel_id=1, source_target_pairs={{0,8},{4,12},{8,0},{12,4},{16,24},{20,28},{24,16},{28,20},{1,9},{5... | collective-permute-start | bytes 884744 | tf_op jit(solution)/shard_map/ppermute | solution.py:456
  95.6 15.8 %collective-permute-start.7 = (bf16[384,768]{1,0:T(8,128)(2,1)S(1)}, bf16[384,768]{1,0:T(8,128)(2,1)S(1)}, u32[]{:S(2)}, u32[]{:S(2)}) collective-permute-start(bf16[384,768]{1,0:T(8,128)(2,1)S(1)} %add_convert_fusion.3), channel_id=1, source_target_pairs={{0,2},{1,3},{2,0},{3,1},{4,6},{5,7},{6,4},{7,5},{8,10},{9,11},{10,... | collective-permute-start | bytes 1769480 | tf_op jit(solution)/shard_map/ppermute | solution.py:456
  97.5 21.3 %collective-permute-start.11 = (bf16[2,2,1,96,768]{4,3,2,1,0:T(8,128)(2,1)}, bf16[2,2,1,96,768]{4,3,2,1,0:T(8,128)(2,1)}, u32[]{:S(2)}, u32[]{:S(2)}) collective-permute-start(bf16[2,2,1,96,768]{4,3,2,1,0:T(8,128)(2,1)} %pad_maximum_fusion.21), channel_id=1, source_target_pairs={{0,4},{4,0},{8,12},{12,8},{16,20},{20,16},{24,28},{28,24},{1,5},{5... | collective-permute-start | bytes 1769480 | tf_op jit(solution)/shard_map/ppermute | solution.py:456
  99.8 26.1 %collective-permute-start.14 = (bf16[2,2,1,96,768]{4,3,2,1,0:T(8,128)(2,1)}, bf16[2,2,1,96,768]{4,3,2,1,0:T(8,128)(2,1)}, u32[]{:S(2)}, u32[]{:S(2)}) collective-permute-start(bf16[2,2,1,96,768]{4,3,2,1,0:T(8,128)(2,1)} %pad_maximum_fusion.22), channel_id=1, source_target_pairs={{0,4},{4,0},{8,12},{12,8},{16,20},{20,16},{24,28},{28,24},{1,5},{5... | collective-permute-start | bytes 1769480 | tf_op jit(solution)/shard_map/ppermute | solution.py:456
  103.7 23.5 %collective-permute-start.18 = (bf16[768,768]{1,0:T(8,128)(2,1)}, bf16[768,768]{1,0:T(8,128)(2,1)}, u32[]{:S(2)}, u32[]{:S(2)}) collective-permute-start(bf16[768,768]{1,0:T(8,128)(2,1)} %pad_maximum_fusion.12), channel_id=1, source_target_pairs={{0,1},{1,0},{2,3},{3,2},{4,5},{5,4},{6,7},{7,6},{8,9},{9,8},{10,11... | collective-permute-start | bytes 3538952 | tf_op jit(solution)/shard_map/ppermute | solution.py:456
  112.8 15.9 %collective-permute-start.8 = (bf16[768,768]{1,0:T(8,128)(2,1)}, bf16[768,768]{1,0:T(8,128)(2,1)}, u32[]{:S(2)}, u32[]{:S(2)}) collective-permute-start(bf16[768,768]{1,0:T(8,128)(2,1)} %pad_maximum_fusion.9), channel_id=1, source_target_pairs={{0,1},{1,0},{2,3},{3,2},{4,5},{5,4},{6,7},{7,6},{8,9},{9,8},{10,11... | collective-permute-start | bytes 3538952 | tf_op jit(solution)/shard_map/ppermute | solution.py:456
  145.5 16.6 %collective-permute-start.30 = (bf16[2,2,96,768]{3,2,0,1:T(8,128)(2,1)}, bf16[2,2,96,768]{3,2,0,1:T(8,128)(2,1)}, u32[]{:S(2)}, u32[]{:S(2)}) collective-permute-start(bf16[2,2,96,768]{3,2,0,1:T(8,128)(2,1)} %fusion.18), channel_id=1, source_target_pairs={{0,4},{4,0},{8,12},{12,8},{16,20},{20,16},{24,28},{28,24},{1,5},{5... | collective-permute-start | bytes 1769480 | tf_op jit(solution)/shard_map/ppermute | solution.py:456
  150.4 22.7 %collective-permute-start.33 = (bf16[2,2,96,768]{3,2,1,0:T(8,128)(2,1)}, bf16[2,2,96,768]{3,2,1,0:T(8,128)(2,1)}, u32[]{:S(2)}, u32[]{:S(2)}) collective-permute-start(bf16[2,2,96,768]{3,2,1,0:T(8,128)(2,1)} %fusion.19), channel_id=1, source_target_pairs={{0,4},{4,0},{8,12},{12,8},{16,20},{20,16},{24,28},{28,24},{1,5},{5... | collective-permute-start | bytes 1769480 | tf_op jit(solution)/shard_map/ppermute | solution.py:456
  155.4 35.8 %collective-permute-start.15 = (bf16[768,768]{1,0:T(8,128)(2,1)}, bf16[768,768]{1,0:T(8,128)(2,1)}, u32[]{:S(2)}, u32[]{:S(2)}) collective-permute-start(bf16[768,768]{1,0:T(8,128)(2,1)} %slice.746), channel_id=1, source_target_pairs={{0,1},{1,0},{2,3},{3,2},{4,5},{5,4},{6,7},{7,6},{8,9},{9,8},{10,11... | collective-permute-start | bytes 3538952 | tf_op jit(solution)/shard_map/ppermute | solution.py:456
  157.7 30.8 %collective-permute-start.19 = (bf16[768,768]{1,0:T(8,128)(2,1)}, bf16[768,768]{1,0:T(8,128)(2,1)}, u32[]{:S(2)}, u32[]{:S(2)}) collective-permute-start(bf16[768,768]{1,0:T(8,128)(2,1)} %slice.745), channel_id=1, source_target_pairs={{0,1},{1,0},{2,3},{3,2},{4,5},{5,4},{6,7},{7,6},{8,9},{9,8},{10,11... | collective-permute-start | bytes 3538952 | tf_op jit(solution)/shard_map/ppermute | solution.py:456
  164.0 11.5 %collective-permute-start.31 = (bf16[2,96,768]{2,1,0:T(8,128)(2,1)S(1)}, bf16[2,96,768]{2,1,0:T(8,128)(2,1)S(1)}, u32[]{:S(2)}, u32[]{:S(2)}) collective-permute-start(bf16[2,96,768]{2,1,0:T(8,128)(2,1)S(1)} %fusion.27), channel_id=1, source_target_pairs={{0,8},{4,12},{8,0},{12,4},{16,24},{20,28},{24,16},{28,20},{1,9},{5... | collective-permute-start | bytes 884744 | tf_op jit(solution)/shard_map/ppermute | solution.py:456
  174.6 10.6 %collective-permute-start.34 = (bf16[2,96,768]{2,1,0:T(8,128)(2,1)S(1)}, bf16[2,96,768]{2,1,0:T(8,128)(2,1)S(1)}, u32[]{:S(2)}, u32[]{:S(2)}) collective-permute-start(bf16[2,96,768]{2,1,0:T(8,128)(2,1)S(1)} %fusion.28), channel_id=1, source_target_pairs={{0,8},{4,12},{8,0},{12,4},{16,24},{20,28},{24,16},{28,20},{1,9},{5... | collective-permute-start | bytes 884744 | tf_op jit(solution)/shard_map/ppermute | solution.py:456
  175.6 12.3 %collective-permute-start.32 = (bf16[96,768]{1,0:T(8,128)(2,1)S(1)}, bf16[96,768]{1,0:T(8,128)(2,1)S(1)}, u32[]{:S(2)}, u32[]{:S(2)}) collective-permute-start(bf16[96,768]{1,0:T(8,128)(2,1)S(1)} %fusion.34), channel_id=1, source_target_pairs={{0,16},{4,20},{8,24},{12,28},{16,0},{20,4},{24,8},{28,12},{1,17},{... | collective-permute-start | bytes 442376 | tf_op jit(solution)/shard_map/ppermute | solution.py:456
  190.2 16.3 %collective-permute-start.20 = (bf16[384,768]{1,0:T(8,128)(2,1)S(1)}, bf16[384,768]{1,0:T(8,128)(2,1)S(1)}, u32[]{:S(2)}, u32[]{:S(2)}) collective-permute-start(bf16[384,768]{1,0:T(8,128)(2,1)S(1)} %slice.748), channel_id=1, source_target_pairs={{0,2},{1,3},{2,0},{3,1},{4,6},{5,7},{6,4},{7,5},{8,10},{9,11},{10,... | collective-permute-start | bytes 1769480 | tf_op jit(solution)/shard_map/ppermute | solution.py:456
  192.9 23.8 %collective-permute-start.16 = (bf16[384,768]{1,0:T(8,128)(2,1)S(1)}, bf16[384,768]{1,0:T(8,128)(2,1)S(1)}, u32[]{:S(2)}, u32[]{:S(2)}) collective-permute-start(bf16[384,768]{1,0:T(8,128)(2,1)S(1)} %slice.749), channel_id=1, source_target_pairs={{0,2},{1,3},{2,0},{3,1},{4,6},{5,7},{6,4},{7,5},{8,10},{9,11},{10,... | collective-permute-start | bytes 1769480 | tf_op jit(solution)/shard_map/ppermute | solution.py:456
  233.2 39.2 %collective-permute-start.36 = (bf16[2,2,97,768]{3,1,2,0:T(2,128)(2,1)}, bf16[2,2,97,768]{3,1,2,0:T(2,128)(2,1)}, u32[]{:S(2)}, u32[]{:S(2)}) collective-permute-start(bf16[2,2,97,768]{3,1,2,0:T(2,128)(2,1)} %copy.245), channel_id=1, source_target_pairs={{0,4},{4,0},{8,12},{12,8},{16,20},{20,16},{24,28},{28,24},{1,5},{5... | collective-permute-start | bytes 1787912 | tf_op jit(solution)/shard_map/ppermute | solution.py:456
  274.5 18.5 %collective-permute-start.37 = (bf16[2,97,768]{2,1,0:T(8,128)(2,1)}, bf16[2,97,768]{2,1,0:T(8,128)(2,1)}, u32[]{:S(2)}, u32[]{:S(2)}) collective-permute-start(bf16[2,97,768]{2,1,0:T(8,128)(2,1)} %fusion.24), channel_id=1, source_target_pairs={{0,8},{4,12},{8,0},{12,4},{16,24},{20,28},{24,16},{28,20},{1,9},{5... | collective-permute-start | bytes 893960 | tf_op jit(solution)/shard_map/ppermute | solution.py:456
  289.0 13.3 %collective-permute-start.25 = (bf16[2,2,97,576]{3,1,2,0:T(2,128)(2,1)S(1)}, bf16[2,2,97,576]{3,1,2,0:T(2,128)(2,1)S(1)}, u32[]{:S(2)}, u32[]{:S(2)}) collective-permute-start(bf16[2,2,97,576]{3,1,2,0:T(2,128)(2,1)S(1)} %fusion.23), channel_id=1, source_target_pairs={{0,4},{4,0},{8,12},{12,8},{16,20},{20,16},{24,28},{28,24},{1,5},{5... | collective-permute-start | bytes 1340936 | tf_op jit(solution)/shard_map/ppermute | solution.py:456
  293.0 40.3 %collective-permute-start.23 = (bf16[768,768]{1,0:T(8,128)(2,1)}, bf16[768,768]{1,0:T(8,128)(2,1)}, u32[]{:S(2)}, u32[]{:S(2)}) collective-permute-start(bf16[768,768]{1,0:T(8,128)(2,1)} %slice.744), channel_id=1, source_target_pairs={{0,1},{1,0},{2,3},{3,2},{4,5},{5,4},{6,7},{7,6},{8,9},{9,8},{10,11... | collective-permute-start | bytes 3538952 | tf_op jit(solution)/shard_map/ppermute | solution.py:456
  294.1 11.8 %collective-permute-start.38 = (bf16[97,768]{1,0:T(8,128)(2,1)S(1)}, bf16[97,768]{1,0:T(8,128)(2,1)S(1)}, u32[]{:S(2)}, u32[]{:S(2)}) collective-permute-start(bf16[97,768]{1,0:T(8,128)(2,1)S(1)} %fusion.33), channel_id=1, source_target_pairs={{0,16},{4,20},{8,24},{12,28},{16,0},{20,4},{24,8},{28,12},{1,17},{... | collective-permute-start | bytes 446984 | tf_op jit(solution)/shard_map/ppermute | solution.py:456
  312.8 15.1 %collective-permute-start.39 = (bf16[289,768]{1,0:T(8,128)(2,1)S(1)}, bf16[289,768]{1,0:T(8,128)(2,1)S(1)}, u32[]{:S(2)}, u32[]{:S(2)}) collective-permute-start(bf16[289,768]{1,0:T(8,128)(2,1)S(1)} %pad_maximum_fusion.26), channel_id=1, source_target_pairs={{0,2},{1,3},{2,0},{3,1},{4,6},{5,7},{6,4},{7,5},{8,10},{9,11},{10,... | collective-permute-start | bytes 1331720 | tf_op jit(solution)/shard_map/ppermute | solution.py:456
  331.2 25.4 %collective-permute-start.40 = (bf16[2,289,768]{2,0,1:T(2,128)(2,1)}, bf16[2,289,768]{2,0,1:T(2,128)(2,1)}, u32[]{:S(2)}, u32[]{:S(2)}) collective-permute-start(bf16[2,289,768]{2,0,1:T(2,128)(2,1)} %copy.251), channel_id=1, source_target_pairs={{0,1},{1,0},{2,3},{3,2},{4,5},{5,4},{6,7},{7,6},{8,9},{9,8},{10,11... | collective-permute-start | bytes 2663432 | tf_op jit(solution)/shard_map/ppermute | solution.py:456
  336.4 15.6 %collective-permute-start.24 = (bf16[384,768]{1,0:T(8,128)(2,1)}, bf16[384,768]{1,0:T(8,128)(2,1)}, u32[]{:S(2)}, u32[]{:S(2)}) collective-permute-start(bf16[384,768]{1,0:T(8,128)(2,1)} %slice.747), channel_id=1, source_target_pairs={{0,2},{1,3},{2,0},{3,1},{4,6},{5,7},{6,4},{7,5},{8,10},{9,11},{10,... | collective-permute-start | bytes 1769480 | tf_op jit(solution)/shard_map/ppermute | solution.py:456
  (96 other events, 572.4 us)
Sparse Core Ops, SparseCore 0:
  28.4 45.3 all-gather.1
